TPU v7x, 32 devices: a whole 2x2x4 slice. The times are simulated.
32 devices in a mesh: gx: 8 (over z, x), gy: 4 (over y, core).
Axes of the slice: x: 2, y: 2, z: 4, core: 2. Of those that a mesh axis runs over, the one named last changes fastest.
Arguments:
- right_side: float32 [1024, 512], P(('gx', 'gy')), may hold values from -6 to 6
- diagonal: float32 [1024, 512], P(('gx', 'gy')), may hold values from 0.5 to 2
- features: float32 [1024, 64, 512], P(('gx', 'gy')), may hold values from -0.078125 to 0.078125
- neighbours: int32 [1024, 27], P(('gx', 'gy')), may hold values from -1 to 1023, as said below
- vertex_features: float32 [64, 32768], P(None, ('gx', 'gy')), may hold values from -0.75 to 0.75
- vertex_bricks: int32 [32768], P(('gx', 'gy')), may hold values from 0 to 1023, as said below
Outputs:
- solution_field: float32 [1024, 512], P(('gx', 'gy'))
- residual: float32 [1024, 512], P(('gx', 'gy'))
- vertex_values: float32 [32768], P(('gx', 'gy'))
Inputs may be any that keep to these rules, and one draw needn't show every extreme that they name: `neighbours`: bricks sit at distinct integer brick coordinates; slot k of a row names the brick at the offset (k // 9 - 1, k // 3 % 3 - 1, k % 3 - 1) from its own, or -1 where no brick is there, so slot 13 names the brick itself and the relation is symmetric. Every brick whose coordinates differ from a brick's by at most two in each direction is held by a device whose gx and gy indices each differ from that brick's holder's by at most one. `vertex_bricks`: vertex n names a brick of its own gx slab: a brick from (n // 4096) * 128 to (n // 4096) * 128 + 127.
All inputs are finite; a program needn't handle non-finite values.
Results may differ from a plain program's by a relative error of at most 0.0002.
Values sent between devices are 32-bit elements; how exact they have to be, the bound alone decides.
A program may use at most 64 MiB of HBM per device.

v0:
```python
import jax
import jax.numpy as jnp
from jax import lax
from jax.sharding import PartitionSpec as P

ITERS = 3


def with_halo(cells, sides, width):
    for axis, dim in sides:
        count = lax.axis_size(axis)
        ends = count - 1
        head = lax.slice_in_dim(cells, 0, width, axis=dim)
        tail = lax.slice_in_dim(cells, cells.shape[dim] - width, cells.shape[dim], axis=dim)
        cells = jnp.concatenate(
            [
                lax.ppermute(tail, axis, [(i, (i + 1) % count) for i in range(ends)]),
                cells,
                lax.ppermute(head, axis, [((i + 1) % count, i) for i in range(ends)]),
            ],
            axis=dim,
        )
    return cells


def coefficient(features, field):
    return jnp.einsum("bfv,bv->bf", features, field, precision=lax.Precision.HIGHEST)


def squares(values):
    return lax.psum(jnp.sum(values * values), ("gx", "gy"))


def per_device(right_side, diagonal, features, neighbours, vertex_features, vertex_bricks):
    nrows = features.shape[0]
    width = features.shape[1]
    across = lax.axis_size("gy")
    row_index = lax.axis_index("gx")
    col_index = lax.axis_index("gy")
    targets = jnp.arange(9 * nrows, dtype=jnp.int32)
    valid = neighbours >= 0
    safe_ids = jnp.where(valid, neighbours, 0)
    owner = safe_ids // nrows
    offset_x = owner // across - row_index + 1
    offset_y = owner % across - col_index + 1
    inside = valid & (offset_x >= 0) & (offset_x < 3) & (offset_y >= 0) & (offset_y < 3)
    position, inside = ((offset_x * 3 + offset_y) * nrows + safe_ids % nrows, inside)
    hits = (position[:, :, None] == targets[None, None, :]) & inside[:, :, None]
    counts = jnp.sum(hits.astype(jnp.float32), axis=1)

    def first_halo(values):
        cycle = with_halo(values.reshape(1, 1, nrows, width), (("gx", 0), ("gy", 1)), 1)
        return cycle.reshape(9 * nrows, width)

    def first_sum(values):
        return jnp.dot(counts, first_halo(values), precision=lax.Precision.HIGHEST)

    solution_field = jnp.zeros_like(right_side)
    residual = right_side
    direction = right_side
    norm_now = squares(residual)
    for step in range(ITERS):
        second_cycle = with_halo(
            first_sum(coefficient(features, direction)).reshape(1, 1, nrows, width),
            (("gx", 0), ("gy", 1)),
            1,
        )
        second = jnp.dot(
            counts, second_cycle.reshape(9 * nrows, width), precision=lax.Precision.HIGHEST
        )
        image = diagonal * direction + jnp.einsum(
            "bfv,bf->bv", features, second, precision=lax.Precision.HIGHEST
        )
        alpha = norm_now / lax.psum(jnp.sum(direction * image), ("gx", "gy"))
        solution_field = solution_field + alpha * direction
        residual = residual - alpha * image
        norm_next = squares(residual)
        direction = residual + norm_next / norm_now * direction
        norm_now = norm_next
    surface = first_sum(coefficient(features, solution_field))
    slab_rows = lax.all_gather(surface, "gy", axis=0, tiled=True)
    local_ids = vertex_bricks - row_index * across * nrows
    picked = jnp.take(slab_rows, local_ids, axis=0)
    vertex_values = jnp.sum(vertex_features * picked.T, axis=0)
    return (solution_field, residual, vertex_values)


def solution(mesh):
    placed = (
        P(("gx", "gy"), None),
        P(("gx", "gy"), None),
        P(("gx", "gy"), None, None),
        P(("gx", "gy"), None),
        P(None, ("gx", "gy")),
        P(("gx", "gy")),
    )
    return jax.shard_map(
        per_device,
        mesh=mesh,
        in_specs=placed,
        out_specs=(P(("gx", "gy"), None), P(("gx", "gy"), None), P(("gx", "gy"))),
        check_vma=False,
    )
```

profile of v0, /device:TPU:0, one launch (start us, length us, event | category | flops | bytes accessed | tf_op | source)
XLA Modules:
  0.0 370.3 jit_solution(636600650359652368)
XLA Ops:
  0.7 5.8 %fusion.8 = f32[32,1,64]{2,1,0:T(1,128)S(1)} fusion(f32[32,64,512]{2,1,0:T(8,128)} %param.8, f32[32,512,1]{1,0,2:T(8,128)} %bitcast.92), kind=kOutput, calls=%fused_computation.25 | convolution fusion | flops 12582912 | bytes 4268032 | tf_op jit(solution)/shard_map/bfv,bv->bf/dot_general | solution.py:27
  6.5 1.3 collective-permute-start.1
  7.8 5.5 %collective-permute-start = (f32[1,1,32,64]{3,2,1,0:T(8,128)S(1)}, f32[1,1,32,64]{3,2,1,0:T(8,128)S(1)}, u32[]{:S(2)}, u32[]{:S(2)}) collective-permute-start(f32[1,1,32,64]{3,2,1,0:T(8,128)S(1)} %bitcast.102), channel_id=1, source_target_pairs={{0,4},{4,8},{8,12},{12,16},{16,20},{20,24},{24,28},{1,5},{5,9},{9,... | collective-permute-start | bytes 24584 | tf_op jit(solution)/shard_map/ppermute | solution.py:17
  13.6 1.1 collective-permute-done
  14.7 1.3 collective-permute-start.3
  16.0 3.0 collective-permute-start.2
  19.0 0.3 convert_reduce_fusion
  19.4 0.5 collective-permute-done.2
  20.1 1.3 collective-permute-start.5
  21.4 5.4 %collective-permute-start.4 = (f32[1,1,32,64]{3,2,1,0:T(8,128)S(1)}, f32[1,1,32,64]{3,2,1,0:T(8,128)S(1)}, u32[]{:S(2)}, u32[]{:S(2)}) collective-permute-start(f32[1,1,32,64]{3,2,1,0:T(8,128)S(1)} %convolution_bitcast_fusion.2), channel_id=1, source_target_pairs={{0,4},{4,8},{8,12},{12,16},{16,20},{20,24},{24,28},{1,5},{5,9},{9,... | collective-permute-start | bytes 24584 | tf_op jit(solution)/shard_map/ppermute | solution.py:17
  26.9 1.4 collective-permute-done.4
  28.3 1.3 collective-permute-start.7
  29.6 3.1 collective-permute-start.6
  32.7 0.9 collective-permute-done.6
  33.8 4.3 %fusion.25 = f32[32,1,512]{2,1,0:T(1,128)S(1)} fusion(f32[32,64,1]{1,2,0:T(1,128)S(1)} %bitcast.117, f32[32,64,512]{2,1,0:T(8,128)} %param.8), kind=kOutput, calls=%fused_computation.78 | convolution fusion | flops 12582912 | bytes 4268032 | tf_op jit(solution)/shard_map/bfv,bf->bv/dot_general | solution.py:71
  38.1 0.6 multiply_reduce_fusion.4
  38.8 48.0 %all-reduce = (f32[]{:T(128)}, f32[]{:T(128)}) all-reduce(f32[]{:T(128)} %get-tuple-element.4, f32[]{:T(128)} %get-tuple-element.3), channel_id=1, replica_groups=mesh['gx'=8,'gy'=4] {'gx','gy'}, use_global_device_ids=true, to_apply=%region_1.2 | all-reduce | flops 2 | bytes 16 | tf_op jit(solution)/shard_map/psum | solution.py:31
  88.1 0.6 multiply_reduce_fusion.3
  88.7 40.8 %psum.44 = f32[]{:T(128)} all-reduce(f32[]{:T(128)} %get-tuple-element.9), channel_id=1, replica_groups=mesh['gx'=8,'gy'=4] {'gx','gy'}, use_global_device_ids=true, to_apply=%region_6.7 | all-reduce | flops 1 | bytes 8 | tf_op jit(solution)/shard_map/psum | solution.py:31
  130.8 5.4 %fusion.6 = f32[32,1,64]{2,1,0:T(1,128)S(1)} fusion(f32[32,64,512]{2,1,0:T(8,128)} %param.8, f32[32,512,1]{1,0,2:T(8,128)S(1)} %bitcast.91), kind=kOutput, calls=%fused_computation.23 | convolution fusion | flops 12582912 | bytes 4268032 | tf_op jit(solution)/shard_map/bfv,bv->bf/dot_general | solution.py:27
  136.3 1.3 collective-permute-start.9
  137.6 4.8 %collective-permute-start.8 = (f32[1,1,32,64]{3,2,1,0:T(8,128)S(1)}, f32[1,1,32,64]{3,2,1,0:T(8,128)S(1)}, u32[]{:S(2)}, u32[]{:S(2)}) collective-permute-start(f32[1,1,32,64]{3,2,1,0:T(8,128)S(1)} %bitcast.114), channel_id=1, source_target_pairs={{0,4},{4,8},{8,12},{12,16},{16,20},{20,24},{24,28},{1,5},{5,9},{9,... | collective-permute-start | bytes 24584 | tf_op jit(solution)/shard_map/ppermute | solution.py:17
  142.4 1.4 collective-permute-done.8
  143.8 1.3 collective-permute-start.11
  145.1 3.0 collective-permute-start.10
  148.2 0.9 collective-permute-done.10
  149.2 1.3 collective-permute-start.13
  150.5 5.4 %collective-permute-start.12 = (f32[1,1,32,64]{3,2,1,0:T(8,128)S(1)}, f32[1,1,32,64]{3,2,1,0:T(8,128)S(1)}, u32[]{:S(2)}, u32[]{:S(2)}) collective-permute-start(f32[1,1,32,64]{3,2,1,0:T(8,128)S(1)} %convolution_bitcast_fusion.1), channel_id=1, source_target_pairs={{0,4},{4,8},{8,12},{12,16},{16,20},{20,24},{24,28},{1,5},{5,9},{9,... | collective-permute-start | bytes 24584 | tf_op jit(solution)/shard_map/ppermute | solution.py:17
  156.0 1.4 collective-permute-done.12
  157.4 1.3 collective-permute-start.15
  158.7 3.4 collective-permute-start.14
  162.1 0.7 collective-permute-done.14
  163.0 2.1 fusion.27
  165.1 0.6 multiply_reduce_fusion.2
  165.8 47.3 %psum.45 = f32[]{:T(128)} all-reduce(f32[]{:T(128)} %multiply_reduce_fusion.2), channel_id=1, replica_groups=mesh['gx'=8,'gy'=4] {'gx','gy'}, use_global_device_ids=true, to_apply=%region_8.9 | all-reduce | flops 1 | bytes 8 | tf_op jit(solution)/shard_map/psum | solution.py:74
  214.4 0.6 multiply_reduce_fusion.1
  215.1 39.7 %psum.46 = f32[]{:T(128)} all-reduce(f32[]{:T(128)} %get-tuple-element.7), channel_id=1, replica_groups=mesh['gx'=8,'gy'=4] {'gx','gy'}, use_global_device_ids=true, to_apply=%region_10.11 | all-reduce | flops 1 | bytes 8 | tf_op jit(solution)/shard_map/psum | solution.py:31
  256.1 5.4 %fusion.4 = f32[32,1,64]{2,1,0:T(1,128)S(1)} fusion(f32[32,64,512]{2,1,0:T(8,128)} %param.8, f32[32,512,1]{1,0,2:T(8,128)S(1)} %fusion.22), kind=kOutput, calls=%fused_computation.21 | convolution fusion | flops 12582912 | bytes 4268032 | tf_op jit(solution)/shard_map/bfv,bv->bf/dot_general | solution.py:27
  261.6 1.3 collective-permute-start.17
  262.9 4.8 %collective-permute-start.16 = (f32[1,1,32,64]{3,2,1,0:T(8,128)S(1)}, f32[1,1,32,64]{3,2,1,0:T(8,128)S(1)}, u32[]{:S(2)}, u32[]{:S(2)}) collective-permute-start(f32[1,1,32,64]{3,2,1,0:T(8,128)S(1)} %bitcast.110), channel_id=1, source_target_pairs={{0,4},{4,8},{8,12},{12,16},{16,20},{20,24},{24,28},{1,5},{5,9},{9,... | collective-permute-start | bytes 24584 | tf_op jit(solution)/shard_map/ppermute | solution.py:17
  267.7 1.4 collective-permute-done.16
  269.1 1.3 collective-permute-start.19
  270.4 3.0 collective-permute-start.18
  273.5 0.9 collective-permute-done.18
  274.5 1.3 collective-permute-start.21
  275.8 5.4 %collective-permute-start.20 = (f32[1,1,32,64]{3,2,1,0:T(8,128)S(1)}, f32[1,1,32,64]{3,2,1,0:T(8,128)S(1)}, u32[]{:S(2)}, u32[]{:S(2)}) collective-permute-start(f32[1,1,32,64]{3,2,1,0:T(8,128)S(1)} %convolution_bitcast_fusion), channel_id=1, source_target_pairs={{0,4},{4,8},{8,12},{12,16},{16,20},{20,24},{24,28},{1,5},{5,9},{9,... | collective-permute-start | bytes 24584 | tf_op jit(solution)/shard_map/ppermute | solution.py:17
  281.3 1.4 collective-permute-done.20
  282.7 1.3 collective-permute-start.23
  284.0 3.2 collective-permute-start.22
  287.2 0.9 collective-permute-done.22
  288.3 2.1 fusion.29
  290.5 0.6 multiply_reduce_fusion
  291.1 47.6 %psum.47 = f32[]{:T(128)} all-reduce(f32[]{:T(128)} %multiply_reduce_fusion), channel_id=1, replica_groups=mesh['gx'=8,'gy'=4] {'gx','gy'}, use_global_device_ids=true, to_apply=%region_12.13 | all-reduce | flops 1 | bytes 8 | tf_op jit(solution)/shard_map/psum | solution.py:74
  340.0 0.7 multiply_subtract_fusion
  340.6 5.3 %fusion.2 = f32[32,1,64]{2,1,0:T(1,128)S(1)} fusion(f32[32,64,512]{2,1,0:T(8,128)} %param.8, f32[32,512,1]{1,0,2:T(8,128)S(1)} %bitcast.100), kind=kOutput, calls=%fused_computation.19 | convolution fusion | flops 12582912 | bytes 4268032 | tf_op jit(solution)/shard_map/bfv,bv->bf/dot_general | solution.py:27
  345.9 1.3 collective-permute-start.25
  347.2 4.8 %collective-permute-start.24 = (f32[1,1,32,64]{3,2,1,0:T(8,128)S(1)}, f32[1,1,32,64]{3,2,1,0:T(8,128)S(1)}, u32[]{:S(2)}, u32[]{:S(2)}) collective-permute-start(f32[1,1,32,64]{3,2,1,0:T(8,128)S(1)} %bitcast.106), channel_id=1, source_target_pairs={{0,4},{4,8},{8,12},{12,16},{16,20},{20,24},{24,28},{1,5},{5,9},{9,... | collective-permute-start | bytes 24584 | tf_op jit(solution)/shard_map/ppermute | solution.py:17
  352.1 1.4 collective-permute-done.24
  353.5 1.3 collective-permute-start.27
  354.8 3.0 collective-permute-start.26
  358.1 0.6 collective-permute-done.26
  358.9 7.6 %all_gather.3 = f32[128,64]{1,0:T(8,128)S(1)} all-gather(f32[32,64]{1,0:T(8,128)S(1)} %fusion.30), channel_id=1, replica_groups=mesh['gx'=8,'gy'=4] {'gy'}, dimensions={0}, use_global_device_ids=true | all-gather | bytes 40960 | tf_op jit(solution)/shard_map/all_gather | solution.py:81
  366.5 2.8 gather_fusion
  369.3 1.0 fusion.1
  (60 shorter events, 2.2 us)
Async XLA Ops:
  0.6 12.7 %copy-start.6 = (s32[32,27]{1,0:T(8,128)S(1)}, s32[32,27]{1,0:T(8,128)}, u32[]{:S(2)}) copy-start(s32[32,27]{1,0:T(8,128)} %param.9) | copy-start | bytes 10372
  0.6 37.5 %copy-start.2 = (f32[32,512]{1,0:T(8,128)S(1)}, f32[32,512]{1,0:T(8,128)}, u32[]{:S(2)}) copy-start(f32[32,512]{1,0:T(8,128)} %param.7) | copy-start | bytes 196612
  0.7 37.5 %copy-start.3 = (f32[32,512]{1,0:T(8,128)S(1)}, f32[32,512]{1,0:T(8,128)}, u32[]{:S(2)}) copy-start(f32[32,512]{1,0:T(8,128)} %param.6) | copy-start | bytes 196612
  6.5 7.1 %collective-permute-start.1 = (f32[1,1,32,64]{3,2,1,0:T(8,128)S(1)}, f32[1,1,32,64]{3,2,1,0:T(8,128)S(1)}, u32[]{:S(2)}, u32[]{:S(2)}) collective-permute-start(f32[1,1,32,64]{3,2,1,0:T(8,128)S(1)} %bitcast.101), channel_id=1, source_target_pairs={{4,0},{8,4},{12,8},{16,12},{20,16},{24,20},{28,24},{5,1},{9,5},{13... | collective-permute-start | bytes 24584 | tf_op jit(solution)/shard_map/ppermute | solution.py:19
  7.8 6.9 %collective-permute-start = (f32[1,1,32,64]{3,2,1,0:T(8,128)S(1)}, f32[1,1,32,64]{3,2,1,0:T(8,128)S(1)}, u32[]{:S(2)}, u32[]{:S(2)}) collective-permute-start(f32[1,1,32,64]{3,2,1,0:T(8,128)S(1)} %bitcast.102), channel_id=1, source_target_pairs={{0,4},{4,8},{8,12},{12,16},{16,20},{20,24},{24,28},{1,5},{5,9},{9,... | collective-permute-start | bytes 24584 | tf_op jit(solution)/shard_map/ppermute | solution.py:17
  14.7 4.6 %collective-permute-start.3 = (f32[3,1,32,64]{3,2,1,0:T(8,128)S(1)}, f32[3,1,32,64]{3,2,1,0:T(8,128)S(1)}, u32[]{:S(2)}, u32[]{:S(2)}) collective-permute-start(f32[3,1,32,64]{3,2,1,0:T(8,128)S(1)} %pad_maximum_fusion.7), channel_id=1, source_target_pairs={{1,0},{2,1},{3,2},{5,4},{6,5},{7,6},{9,8},{10,9},{11,10},{13,12},{... | collective-permute-start | bytes 73736 | tf_op jit(solution)/shard_map/ppermute | solution.py:19
  16.0 3.9 %collective-permute-start.2 = (f32[3,1,32,64]{3,2,1,0:T(8,128)S(1)}, f32[3,1,32,64]{3,2,1,0:T(8,128)S(1)}, u32[]{:S(2)}, u32[]{:S(2)}) collective-permute-start(f32[3,1,32,64]{3,2,1,0:T(8,128)S(1)} %pad_maximum_fusion.7), channel_id=1, source_target_pairs={{0,1},{1,2},{2,3},{4,5},{5,6},{6,7},{8,9},{9,10},{10,11},{12,13},{... | collective-permute-start | bytes 73736 | tf_op jit(solution)/shard_map/ppermute | solution.py:17
  20.1 6.8 %collective-permute-start.5 = (f32[1,1,32,64]{3,2,1,0:T(8,128)S(1)}, f32[1,1,32,64]{3,2,1,0:T(8,128)S(1)}, u32[]{:S(2)}, u32[]{:S(2)}) collective-permute-start(f32[1,1,32,64]{3,2,1,0:T(8,128)S(1)} %convolution_bitcast_fusion.2), channel_id=1, source_target_pairs={{4,0},{8,4},{12,8},{16,12},{20,16},{24,20},{28,24},{5,1},{9,5},{13... | collective-permute-start | bytes 24584 | tf_op jit(solution)/shard_map/ppermute | solution.py:19
  21.4 6.9 %collective-permute-start.4 = (f32[1,1,32,64]{3,2,1,0:T(8,128)S(1)}, f32[1,1,32,64]{3,2,1,0:T(8,128)S(1)}, u32[]{:S(2)}, u32[]{:S(2)}) collective-permute-start(f32[1,1,32,64]{3,2,1,0:T(8,128)S(1)} %convolution_bitcast_fusion.2), channel_id=1, source_target_pairs={{0,4},{4,8},{8,12},{12,16},{16,20},{20,24},{24,28},{1,5},{5,9},{9,... | collective-permute-start | bytes 24584 | tf_op jit(solution)/shard_map/ppermute | solution.py:17
  28.3 4.4 %collective-permute-start.7 = (f32[3,1,32,64]{3,2,1,0:T(8,128)S(1)}, f32[3,1,32,64]{3,2,1,0:T(8,128)S(1)}, u32[]{:S(2)}, u32[]{:S(2)}) collective-permute-start(f32[3,1,32,64]{3,2,1,0:T(8,128)S(1)} %pad_maximum_fusion.8), channel_id=1, source_target_pairs={{1,0},{2,1},{3,2},{5,4},{6,5},{7,6},{9,8},{10,9},{11,10},{13,12},{... | collective-permute-start | bytes 73736 | tf_op jit(solution)/shard_map/ppermute | solution.py:19
  29.6 4.0 %collective-permute-start.6 = (f32[3,1,32,64]{3,2,1,0:T(8,128)S(1)}, f32[3,1,32,64]{3,2,1,0:T(8,128)S(1)}, u32[]{:S(2)}, u32[]{:S(2)}) collective-permute-start(f32[3,1,32,64]{3,2,1,0:T(8,128)S(1)} %pad_maximum_fusion.8), channel_id=1, source_target_pairs={{0,1},{1,2},{2,3},{4,5},{5,6},{6,7},{8,9},{9,10},{10,11},{12,13},{... | collective-permute-start | bytes 73736 | tf_op jit(solution)/shard_map/ppermute | solution.py:17
  130.8 32.2 %copy-start = (f32[32,64,512]{2,1,0:T(8,128)S(1)}, f32[32,64,512]{2,1,0:T(8,128)}, u32[]{:S(2)}) copy-start(f32[32,64,512]{2,1,0:T(8,128)} %param.8) | copy-start | bytes 12582916
  136.3 6.1 %collective-permute-start.9 = (f32[1,1,32,64]{3,2,1,0:T(8,128)S(1)}, f32[1,1,32,64]{3,2,1,0:T(8,128)S(1)}, u32[]{:S(2)}, u32[]{:S(2)}) collective-permute-start(f32[1,1,32,64]{3,2,1,0:T(8,128)S(1)} %bitcast.113), channel_id=1, source_target_pairs={{4,0},{8,4},{12,8},{16,12},{20,16},{24,20},{28,24},{5,1},{9,5},{13... | collective-permute-start | bytes 24584 | tf_op jit(solution)/shard_map/ppermute | solution.py:19
  137.6 6.2 %collective-permute-start.8 = (f32[1,1,32,64]{3,2,1,0:T(8,128)S(1)}, f32[1,1,32,64]{3,2,1,0:T(8,128)S(1)}, u32[]{:S(2)}, u32[]{:S(2)}) collective-permute-start(f32[1,1,32,64]{3,2,1,0:T(8,128)S(1)} %bitcast.114), channel_id=1, source_target_pairs={{0,4},{4,8},{8,12},{12,16},{16,20},{20,24},{24,28},{1,5},{5,9},{9,... | collective-permute-start | bytes 24584 | tf_op jit(solution)/shard_map/ppermute | solution.py:17
  143.8 4.3 %collective-permute-start.11 = (f32[3,1,32,64]{3,2,1,0:T(8,128)S(1)}, f32[3,1,32,64]{3,2,1,0:T(8,128)S(1)}, u32[]{:S(2)}, u32[]{:S(2)}) collective-permute-start(f32[3,1,32,64]{3,2,1,0:T(8,128)S(1)} %pad_maximum_fusion.9), channel_id=1, source_target_pairs={{1,0},{2,1},{3,2},{5,4},{6,5},{7,6},{9,8},{10,9},{11,10},{13,12},{... | collective-permute-start | bytes 73736 | tf_op jit(solution)/shard_map/ppermute | solution.py:19
  145.1 3.9 %collective-permute-start.10 = (f32[3,1,32,64]{3,2,1,0:T(8,128)S(1)}, f32[3,1,32,64]{3,2,1,0:T(8,128)S(1)}, u32[]{:S(2)}, u32[]{:S(2)}) collective-permute-start(f32[3,1,32,64]{3,2,1,0:T(8,128)S(1)} %pad_maximum_fusion.9), channel_id=1, source_target_pairs={{0,1},{1,2},{2,3},{4,5},{5,6},{6,7},{8,9},{9,10},{10,11},{12,13},{... | collective-permute-start | bytes 73736 | tf_op jit(solution)/shard_map/ppermute | solution.py:17
  149.2 6.8 %collective-permute-start.13 = (f32[1,1,32,64]{3,2,1,0:T(8,128)S(1)}, f32[1,1,32,64]{3,2,1,0:T(8,128)S(1)}, u32[]{:S(2)}, u32[]{:S(2)}) collective-permute-start(f32[1,1,32,64]{3,2,1,0:T(8,128)S(1)} %convolution_bitcast_fusion.1), channel_id=1, source_target_pairs={{4,0},{8,4},{12,8},{16,12},{20,16},{24,20},{28,24},{5,1},{9,5},{13... | collective-permute-start | bytes 24584 | tf_op jit(solution)/shard_map/ppermute | solution.py:19
  150.5 6.9 %collective-permute-start.12 = (f32[1,1,32,64]{3,2,1,0:T(8,128)S(1)}, f32[1,1,32,64]{3,2,1,0:T(8,128)S(1)}, u32[]{:S(2)}, u32[]{:S(2)}) collective-permute-start(f32[1,1,32,64]{3,2,1,0:T(8,128)S(1)} %convolution_bitcast_fusion.1), channel_id=1, source_target_pairs={{0,4},{4,8},{8,12},{12,16},{16,20},{20,24},{24,28},{1,5},{5,9},{9,... | collective-permute-start | bytes 24584 | tf_op jit(solution)/shard_map/ppermute | solution.py:17
  157.4 4.7 %collective-permute-start.15 = (f32[3,1,32,64]{3,2,1,0:T(8,128)S(1)}, f32[3,1,32,64]{3,2,1,0:T(8,128)S(1)}, u32[]{:S(2)}, u32[]{:S(2)}) collective-permute-start(f32[3,1,32,64]{3,2,1,0:T(8,128)S(1)} %pad_maximum_fusion.10), channel_id=1, source_target_pairs={{1,0},{2,1},{3,2},{5,4},{6,5},{7,6},{9,8},{10,9},{11,10},{13,12},{... | collective-permute-start | bytes 73736 | tf_op jit(solution)/shard_map/ppermute | solution.py:19
  158.7 4.1 %collective-permute-start.14 = (f32[3,1,32,64]{3,2,1,0:T(8,128)S(1)}, f32[3,1,32,64]{3,2,1,0:T(8,128)S(1)}, u32[]{:S(2)}, u32[]{:S(2)}) collective-permute-start(f32[3,1,32,64]{3,2,1,0:T(8,128)S(1)} %pad_maximum_fusion.10), channel_id=1, source_target_pairs={{0,1},{1,2},{2,3},{4,5},{5,6},{6,7},{8,9},{9,10},{10,11},{12,13},{... | collective-permute-start | bytes 73736 | tf_op jit(solution)/shard_map/ppermute | solution.py:17
  256.1 32.2 %copy-start.1 = (f32[32,64,512]{2,1,0:T(8,128)S(1)}, f32[32,64,512]{2,1,0:T(8,128)}, u32[]{:S(2)}) copy-start(f32[32,64,512]{2,1,0:T(8,128)} %param.8) | copy-start | bytes 12582916
  261.6 6.1 %collective-permute-start.17 = (f32[1,1,32,64]{3,2,1,0:T(8,128)S(1)}, f32[1,1,32,64]{3,2,1,0:T(8,128)S(1)}, u32[]{:S(2)}, u32[]{:S(2)}) collective-permute-start(f32[1,1,32,64]{3,2,1,0:T(8,128)S(1)} %bitcast.109), channel_id=1, source_target_pairs={{4,0},{8,4},{12,8},{16,12},{20,16},{24,20},{28,24},{5,1},{9,5},{13... | collective-permute-start | bytes 24584 | tf_op jit(solution)/shard_map/ppermute | solution.py:19
  262.9 6.2 %collective-permute-start.16 = (f32[1,1,32,64]{3,2,1,0:T(8,128)S(1)}, f32[1,1,32,64]{3,2,1,0:T(8,128)S(1)}, u32[]{:S(2)}, u32[]{:S(2)}) collective-permute-start(f32[1,1,32,64]{3,2,1,0:T(8,128)S(1)} %bitcast.110), channel_id=1, source_target_pairs={{0,4},{4,8},{8,12},{12,16},{16,20},{20,24},{24,28},{1,5},{5,9},{9,... | collective-permute-start | bytes 24584 | tf_op jit(solution)/shard_map/ppermute | solution.py:17
  269.1 4.3 %collective-permute-start.19 = (f32[3,1,32,64]{3,2,1,0:T(8,128)S(1)}, f32[3,1,32,64]{3,2,1,0:T(8,128)S(1)}, u32[]{:S(2)}, u32[]{:S(2)}) collective-permute-start(f32[3,1,32,64]{3,2,1,0:T(8,128)S(1)} %pad_maximum_fusion.11), channel_id=1, source_target_pairs={{1,0},{2,1},{3,2},{5,4},{6,5},{7,6},{9,8},{10,9},{11,10},{13,12},{... | collective-permute-start | bytes 73736 | tf_op jit(solution)/shard_map/ppermute | solution.py:19
  270.4 3.9 %collective-permute-start.18 = (f32[3,1,32,64]{3,2,1,0:T(8,128)S(1)}, f32[3,1,32,64]{3,2,1,0:T(8,128)S(1)}, u32[]{:S(2)}, u32[]{:S(2)}) collective-permute-start(f32[3,1,32,64]{3,2,1,0:T(8,128)S(1)} %pad_maximum_fusion.11), channel_id=1, source_target_pairs={{0,1},{1,2},{2,3},{4,5},{5,6},{6,7},{8,9},{9,10},{10,11},{12,13},{... | collective-permute-start | bytes 73736 | tf_op jit(solution)/shard_map/ppermute | solution.py:17
  274.5 6.8 %collective-permute-start.21 = (f32[1,1,32,64]{3,2,1,0:T(8,128)S(1)}, f32[1,1,32,64]{3,2,1,0:T(8,128)S(1)}, u32[]{:S(2)}, u32[]{:S(2)}) collective-permute-start(f32[1,1,32,64]{3,2,1,0:T(8,128)S(1)} %convolution_bitcast_fusion), channel_id=1, source_target_pairs={{4,0},{8,4},{12,8},{16,12},{20,16},{24,20},{28,24},{5,1},{9,5},{13... | collective-permute-start | bytes 24584 | tf_op jit(solution)/shard_map/ppermute | solution.py:19
  275.8 6.9 %collective-permute-start.20 = (f32[1,1,32,64]{3,2,1,0:T(8,128)S(1)}, f32[1,1,32,64]{3,2,1,0:T(8,128)S(1)}, u32[]{:S(2)}, u32[]{:S(2)}) collective-permute-start(f32[1,1,32,64]{3,2,1,0:T(8,128)S(1)} %convolution_bitcast_fusion), channel_id=1, source_target_pairs={{0,4},{4,8},{8,12},{12,16},{16,20},{20,24},{24,28},{1,5},{5,9},{9,... | collective-permute-start | bytes 24584 | tf_op jit(solution)/shard_map/ppermute | solution.py:17
  282.7 4.5 %collective-permute-start.23 = (f32[3,1,32,64]{3,2,1,0:T(8,128)S(1)}, f32[3,1,32,64]{3,2,1,0:T(8,128)S(1)}, u32[]{:S(2)}, u32[]{:S(2)}) collective-permute-start(f32[3,1,32,64]{3,2,1,0:T(8,128)S(1)} %pad_maximum_fusion.12), channel_id=1, source_target_pairs={{1,0},{2,1},{3,2},{5,4},{6,5},{7,6},{9,8},{10,9},{11,10},{13,12},{... | collective-permute-start | bytes 73736 | tf_op jit(solution)/shard_map/ppermute | solution.py:19
  284.0 4.1 %collective-permute-start.22 = (f32[3,1,32,64]{3,2,1,0:T(8,128)S(1)}, f32[3,1,32,64]{3,2,1,0:T(8,128)S(1)}, u32[]{:S(2)}, u32[]{:S(2)}) collective-permute-start(f32[3,1,32,64]{3,2,1,0:T(8,128)S(1)} %pad_maximum_fusion.12), channel_id=1, source_target_pairs={{0,1},{1,2},{2,3},{4,5},{5,6},{6,7},{8,9},{9,10},{10,11},{12,13},{... | collective-permute-start | bytes 73736 | tf_op jit(solution)/shard_map/ppermute | solution.py:17
  288.3 63.7 %copy-start.7 = (s32[1024]{0:T(1024)S(1)}, s32[1024]{0:T(1024)}, u32[]{:S(2)}) copy-start(s32[1024]{0:T(1024)} %param.11) | copy-start | bytes 12292
  288.3 69.5 %copy-start.5 = (f32[64,1024]{1,0:T(8,128)S(1)}, f32[64,1024]{1,0:T(8,128)}, u32[]{:S(2)}) copy-start(f32[64,1024]{1,0:T(8,128)} %param.10) | copy-start | bytes 786436
  340.6 28.7 %copy-start.4 = (f32[32,512]{1,0:T(8,128)}, f32[32,512]{1,0:T(8,128)S(1)}, u32[]{:S(2)}) copy-start(f32[32,512]{1,0:T(8,128)S(1)} %get-tuple-element.12) | copy-start | bytes 196612
  345.9 6.1 %collective-permute-start.25 = (f32[1,1,32,64]{3,2,1,0:T(8,128)S(1)}, f32[1,1,32,64]{3,2,1,0:T(8,128)S(1)}, u32[]{:S(2)}, u32[]{:S(2)}) collective-permute-start(f32[1,1,32,64]{3,2,1,0:T(8,128)S(1)} %bitcast.105), channel_id=1, source_target_pairs={{4,0},{8,4},{12,8},{16,12},{20,16},{24,20},{28,24},{5,1},{9,5},{13... | collective-permute-start | bytes 24584 | tf_op jit(solution)/shard_map/ppermute | solution.py:19
  347.2 6.2 %collective-permute-start.24 = (f32[1,1,32,64]{3,2,1,0:T(8,128)S(1)}, f32[1,1,32,64]{3,2,1,0:T(8,128)S(1)}, u32[]{:S(2)}, u32[]{:S(2)}) collective-permute-start(f32[1,1,32,64]{3,2,1,0:T(8,128)S(1)} %bitcast.106), channel_id=1, source_target_pairs={{0,4},{4,8},{8,12},{12,16},{16,20},{20,24},{24,28},{1,5},{5,9},{9,... | collective-permute-start | bytes 24584 | tf_op jit(solution)/shard_map/ppermute | solution.py:17
  353.5 4.6 %collective-permute-start.27 = (f32[3,1,32,64]{3,2,1,0:T(8,128)S(1)}, f32[3,1,32,64]{3,2,1,0:T(8,128)S(1)}, u32[]{:S(2)}, u32[]{:S(2)}) collective-permute-start(f32[3,1,32,64]{3,2,1,0:T(8,128)S(1)} %pad_maximum_fusion.13), channel_id=1, source_target_pairs={{1,0},{2,1},{3,2},{5,4},{6,5},{7,6},{9,8},{10,9},{11,10},{13,12},{... | collective-permute-start | bytes 73736 | tf_op jit(solution)/shard_map/ppermute | solution.py:19
  354.8 3.9 %collective-permute-start.26 = (f32[3,1,32,64]{3,2,1,0:T(8,128)S(1)}, f32[3,1,32,64]{3,2,1,0:T(8,128)S(1)}, u32[]{:S(2)}, u32[]{:S(2)}) collective-permute-start(f32[3,1,32,64]{3,2,1,0:T(8,128)S(1)} %pad_maximum_fusion.13), channel_id=1, source_target_pairs={{0,1},{1,2},{2,3},{4,5},{5,6},{6,7},{8,9},{9,10},{10,11},{12,13},{... | collective-permute-start | bytes 73736 | tf_op jit(solution)/shard_map/ppermute | solution.py:17
where the time goes:
time: 374 us; the launch traced here: 370 us
  blocking collectives  231 us (62%)
  starting transfers between devices  76 us (20%)
  matrix products  32 us (9%)
  waiting for transfers between devices  14.9 us (4%)
  between operations  7.94 us (2%)
  other arithmetic  5.32 us (1%)
    psum x3, blocking collectives, squares(): return lax.psum(jnp.sum(values * values), ('gx', 'gy'))  128 us
    psum x2, blocking collectives, per_device(): alpha = norm_now / lax.psum(jnp.sum(direction * image), ('gx', 'gy'))  94.9 us
    ppermute x14, starting transfers between devices, with_halo(): lax.ppermute(tail, axis, [(i, (i + 1) % count) for i in range(ends)])  58 us
    dot_general x4, matrix products, coefficient(): jnp.einsum('bfv,bv->bf', features, field, precision=lax.Precision.HIGHEST)  22 us
    ppermute x14, starting transfers between devices, with_halo(): lax.ppermute(head, axis, [((i + 1) % count, i) for i in range(ends)])  18 us
    ppermute x14, waiting for transfers between devices, with_halo(): lax.ppermute(tail, axis, [(i, (i + 1) % count) for i in range(ends)])  14.8 us
    dot_general x3, matrix products, per_device(): jnp.einsum('bfv,bf->bv', features, second, precision=lax.Precision.HIGHEST)  8.5 us
    all_gather x1, blocking collectives, per_device(): slab_rows = lax.all_gather(surface, 'gy', axis=0, tiled=True)  7.56 us
  transfers between devices with their start and end apart: 28, of which 14 were waited for; matrix products, arithmetic and copies ran while one was open for 0% of the time, Pallas kernels for 0%

commit v1 on v0

v1 whole, which is shorter than its diff:
```python
import functools

import jax
import jax.numpy as jnp
from jax import lax
from jax.experimental import pallas as pl
from jax.experimental.pallas import tpu as pltpu
from jax.sharding import PartitionSpec as P

ITERS = 3
CHUNKS = 4
MESH = pl.DeviceIdType.MESH
F32 = jnp.float32
BF16 = jnp.bfloat16


def split3(x):
    hi = x.astype(BF16)
    rest = x - hi.astype(F32)
    mid = rest.astype(BF16)
    lo = (rest - mid.astype(F32)).astype(BF16)
    return hi, mid, lo


def iota(shape, dim):
    return lax.broadcasted_iota(jnp.int32, shape, dim)


def kernel(
    along, across, nrows, width, slots,
    b_hbm, d_hbm, f_hbm, nb_ref, vf_hbm, vb_ref,
    x_ref, r_ref, out_ref,
    b_ref, d_ref, f_ref, vf_ref, dr_ref, p_ref, s_ref, w_ref,
    tab, win, slab, sums, nwin, a4, onehot,
    load_sem, tab_send, tab_recv, win_send, win_recv, slab_send, slab_recv, sum_send, sum_recv,
):
    half = nrows // 2
    wrows = 9 * half
    count = along * across
    gx = lax.axis_index("gx")
    gy = lax.axis_index("gy")
    me = gx * across + gy
    log_rows = nrows.bit_length() - 1
    log_across = across.bit_length() - 1

    step = nrows // CHUNKS
    load_b = pltpu.make_async_copy(b_hbm, b_ref, load_sem.at[0])
    load_d = pltpu.make_async_copy(d_hbm, d_ref, load_sem.at[1])
    load_vf = pltpu.make_async_copy(vf_hbm, vf_ref, load_sem.at[2])
    load_f = [
        pltpu.make_async_copy(
            f_hbm.at[pl.ds(c * step, step)], f_ref.at[pl.ds(c * step, step)], load_sem.at[3 + c]
        )
        for c in range(CHUNKS)
    ]
    load_b.start()
    for copy in load_f:
        copy.start()
    load_d.start()
    load_vf.start()

    tab[...] = jnp.full(tab.shape, -1, jnp.int32)
    win[...] = jnp.zeros(win.shape, F32)

    barrier = pltpu.get_barrier_semaphore()

    def peer(p):
        dev = lax.rem(me + p, count)
        return (dev // across, lax.rem(dev, across))

    def over_peers(body):
        if count <= 32:
            for p in range(1, count):
                body(p)
        else:
            def wrapped(p, carry):
                body(p)
                return carry
            lax.fori_loop(1, count, wrapped, 0)

    def greet(p):
        pl.semaphore_signal(barrier, inc=1, device_id=peer(p), device_id_type=MESH)

    over_peers(greet)

    places = []
    for q in range(9):
        if q != 4:
            dx, dy = q // 3 - 1, q % 3 - 1
            there = (gx + dx >= 0) & (gx + dx < along) & (gy + dy >= 0) & (gy + dy < across)
            places.append((q, there, (gx + dx, gy + dy)))

    def halo(buf, send, recv):
        def copy(q, device):
            return pltpu.make_async_remote_copy(
                src_ref=buf.at[4], dst_ref=buf.at[8 - q], send_sem=send.at[q],
                recv_sem=recv.at[8 - q], device_id=device, device_id_type=MESH,
            )

        def arrive(q, device):
            return pltpu.make_async_remote_copy(
                src_ref=buf.at[4], dst_ref=buf.at[q], send_sem=send.at[q],
                recv_sem=recv.at[q], device_id=device, device_id_type=MESH,
            )

        def start():
            for q, there, device in places:
                pl.when(there)(lambda q=q, device=device: copy(q, device).start())

        def wait_recv():
            for q, there, device in places:
                pl.when(there)(lambda q=q, device=device: arrive(q, device).wait_recv())

        def wait_send():
            for q, there, device in places:
                pl.when(there)(lambda q=q, device=device: copy(q, device).wait_send())

        return start, wait_recv, wait_send

    def localize(ids):
        owner = jnp.right_shift(ids, log_rows)
        ox = jnp.right_shift(owner, log_across) - gx + 1
        oy = jnp.bitwise_and(owner, across - 1) - gy + 1
        inside = (ids >= 0) & (ox >= 0) & (ox < 3) & (oy >= 0) & (oy < 3)
        row = jnp.bitwise_and(ids, nrows - 1)
        spot = jnp.where(row >= half, wrows - half, 0) + (ox * 3 + oy) * half + row
        return jnp.where(inside, spot, -1)

    own = nb_ref[...]
    own_t = jnp.transpose(own)
    tab[4, 0:slots, :] = jnp.concatenate([own_t] * (128 // nrows), axis=1)

    pl.semaphore_wait(barrier, count - 1)
    tab_start, tab_wait, tab_done = halo(tab, tab_send, tab_recv)
    tab_start()

    spots = localize(own)
    lanes2 = iota((nrows, wrows), 1)
    n_even = jnp.zeros((nrows, wrows), F32)
    n_odd = jnp.zeros((nrows, wrows), F32)
    for k in range(slots):
        col = spots[:, k:k + 1]
        n_even = jnp.where(col == lanes2, 1.0, n_even)
        n_odd = jnp.where(col == lanes2 + wrows, 1.0, n_odd)
    a4[2 * nrows:3 * nrows, :] = n_even.astype(BF16)
    a4[3 * nrows:4 * nrows, :] = n_odd.astype(BF16)

    load_b.wait()
    lane = iota((width, 128), 1)

    def reduce_coeff(b, rows, acc):
        prod = f_ref[b] * rows
        part = prod[:, 0:128]
        for j in range(1, prod.shape[1] // 128):
            part = part + prod[:, j * 128:(j + 1) * 128]
        total = jnp.sum(part, axis=1, keepdims=True)
        h, i = b // half, b % half
        acc[h] = jnp.where(lane == i, total, acc[h])

    def pack(acc):
        both = jnp.concatenate(acc, axis=0)
        return jnp.transpose(both)[0:half, :]

    acc = [jnp.zeros((width, 128), F32)] * 2
    for c in range(CHUNKS):
        load_f[c].wait()
        for b in range(c * step, (c + 1) * step):
            reduce_coeff(b, b_ref[b:b + 1, :], acc)
    win[0, 4] = pack(acc)
    win_ops = [halo(win.at[k], win_send.at[k], win_recv.at[k]) for k in range(ITERS)]
    win_ops[0][0]()

    vb = vb_ref[...] - gx * (across * nrows)
    vrow = jnp.bitwise_and(vb, nrows - 1)
    code = (
        jnp.where(vrow >= half, across * half - half, 0)
        + jnp.right_shift(vb, log_rows) * half + vrow
    )
    for g in range(across * nrows // 16):
        block = iota((16, vb.shape[1]), 0) + 16 * g
        onehot[16 * g:16 * (g + 1), :] = jnp.where(block == code, 1.0, 0.0).astype(BF16)

    nwin[...] = jnp.zeros(nwin.shape, BF16)
    tab_wait()
    group = iota((slots, 128), 1) // nrows
    for ox in range(3):
        ids = jnp.where(
            group == 0, tab[3 * ox, 0:slots, :],
            jnp.where(group == 1, tab[3 * ox + 1, 0:slots, :], tab[3 * ox + 2, 0:slots, :]),
        )
        target = jnp.where(group < 3, localize(ids), -1)
        rows = [jnp.broadcast_to(target[k:k + 1, :], (16, 128)) for k in range(slots)]
        low, high = ((0, 6), (0, 9), (3, 9))[ox]
        per = (high - low) * half // 16

        def build(g, carry, rows=rows, low=low, per=per, ox=ox):
            h = g // per
            start = pl.multiple_of(h * wrows + low * half + (g - h * per) * 16, 16)
            spot = iota((16, 128), 0) + start
            hits = jnp.zeros((16, 128), F32)
            for row in rows:
                hits = jnp.where(row == spot, 1.0, hits)
            nwin[pl.ds(start, 16), ox * 128:(ox + 1) * 128] = hits.astype(BF16)
            return carry

        lax.fori_loop(0, 2 * per, build, 0)
    n_loc = jnp.concatenate(
        [nwin[4 * half:5 * half, :], nwin[wrows + 4 * half:wrows + 5 * half, :]], axis=0
    )
    for h in range(2):
        two = lax.dot_general(
            n_loc, nwin[h * wrows:(h + 1) * wrows, :], (((1,), (1,)), ((), ())),
            preferred_element_type=F32,
        )
        a4[h * nrows:(h + 1) * nrows, :] = two.astype(BF16)
    load_d.wait()

    low_lanes = iota((nrows, 128), 1) < width
    ar_rows = iota((8, 128), 0)
    ar_lanes = iota((8, 128), 1)

    def fold(x):
        tot = x[0:8, :]
        for i in range(1, x.shape[0] // 8):
            tot = tot + x[8 * i:8 * (i + 1), :]
        res = tot[:, 0:128]
        for j in range(1, x.shape[1] // 128):
            res = res + tot[:, 128 * j:128 * (j + 1)]
        return jnp.sum(res, axis=0, keepdims=True)

    r = b_ref[...]
    beta = None
    firsts = []
    alphas, betas = [], []
    for it in range(ITERS):
        dr = d_ref[...] * r
        dr_ref[...] = dr
        gamma_part = fold(r * r)
        delta_part = fold(r * dr)
        mu_part = fold(r * s_ref[...]) if it else jnp.zeros((1, 128), F32)
        if it == 0:
            win_ops[0][1]()
            cr = win[0].reshape(wrows, 2 * width)
        parts = jnp.concatenate(split3(cr), axis=1)
        prod = jnp.dot(a4[...], parts, preferred_element_type=F32)
        prod = prod[:, 0:128] + prod[:, 128:256] + prod[:, 256:384]
        second = prod[0:nrows] + pltpu.roll(prod[nrows:2 * nrows], width, 1)
        first = prod[2 * nrows:3 * nrows] + pltpu.roll(prod[3 * nrows:], width, 1)
        delta_part = delta_part + fold(jnp.where(low_lanes, first * first, 0.0))
        three = jnp.where(
            ar_rows == 0, gamma_part, jnp.where(ar_rows == 1, delta_part, mu_part)
        )
        three = jnp.sum(three, axis=1, keepdims=True)
        sums[it, me] = jnp.sum(
            jnp.where((ar_rows == ar_lanes) & (ar_rows < 3), three, 0.0), axis=0, keepdims=True
        )

        def send_sum(p, it=it):
            pltpu.make_async_remote_copy(
                src_ref=sums.at[it, me], dst_ref=sums.at[it, me], send_sem=sum_send.at[it],
                recv_sem=sum_recv.at[it], device_id=peer(p), device_id_type=MESH,
            ).start()

        over_peers(send_sum)

        slab[it, gy] = jnp.where(
            low_lanes[0:half], first[0:half], pltpu.roll(first[half:], width, 1)
        )
        for p in range(1, across):
            pltpu.make_async_remote_copy(
                src_ref=slab.at[it, gy], dst_ref=slab.at[it, gy], send_sem=slab_send.at[it],
                recv_sem=slab_recv.at[it], device_id=(gx, lax.rem(gy + p, across)),
                device_id_type=MESH,
            ).start()

        second_t = jnp.transpose(second)[0:width, :]
        acc = [jnp.zeros((width, 128), F32)] * 2
        for b in range(nrows):
            g = jnp.sum(f_ref[b] * second_t[:, b:b + 1], axis=0, keepdims=True)
            row = dr_ref[b:b + 1, :] + g
            w_ref[b:b + 1, :] = row
            if it < ITERS - 1:
                reduce_coeff(b, row, acc)
        if it < ITERS - 1:
            win[it + 1, 4] = pack(acc)
            win_ops[it + 1][0]()
        else:
            load_vf.wait()
            for k in range(ITERS):
                pltpu.make_async_copy(
                    slab.at[k, pl.ds(0, across - 1)], slab.at[k, pl.ds(0, across - 1)],
                    slab_recv.at[k],
                ).wait()
            pieces = [slab[k].reshape(across * half, 2 * width) for k in range(ITERS)]
            old = pieces[1] + betas[1] * pieces[0]
            known = alphas[0] * pieces[0] + alphas[1] * old
            vert = []
            for piece in (known, pieces[2], old):
                turned = jnp.transpose(piece)
                turned = jnp.concatenate([turned[0:width], turned[width:]], axis=1)
                hi = turned.astype(BF16)
                lo = (turned - hi.astype(F32)).astype(BF16)
                both = jnp.dot(
                    jnp.concatenate([hi, lo], axis=0), onehot[...], preferred_element_type=F32
                )
                vert.append(jnp.sum(
                    (both[0:width] + both[width:]) * vf_ref[...], axis=0, keepdims=True
                ))

        pltpu.make_async_copy(
            sums.at[it, pl.ds(0, count - 1)], sums.at[it, pl.ds(0, count - 1)], sum_recv.at[it]
        ).wait()
        total = jnp.sum(sums[it], axis=0)
        gamma, delta, mu = total[:, 0:1], total[:, 1:2], total[:, 2:3]
        if it == 0:
            energy = delta
        else:
            beta = gamma / gamma_old
            energy = delta + beta * (2.0 * mu + beta * energy)
        alpha = gamma / energy
        gamma_old = gamma
        alphas.append(alpha)
        betas.append(beta)
        if it < ITERS - 1:
            win_ops[it + 1][1]()
            cw = win[it + 1].reshape(wrows, 2 * width)
            cs = cw if it == 0 else cw + beta * cs
            cr = cr - alpha * cs
        w = w_ref[...]
        if it == 0:
            p, s = r, w
            x = alpha * p
        else:
            p = r + beta * p_ref[...]
            s = w + beta * s_ref[...]
            x = x_ref[...] + alpha * p
        r = r - alpha * s
        x_ref[...] = x
        if it < ITERS - 1:
            p_ref[...] = p
            s_ref[...] = s
    r_ref[...] = r
    out_ref[...] = vert[0] + alphas[2] * (vert[1] + betas[2] * vert[2])

    tab_done()
    for it in range(ITERS):
        win_ops[it][2]()
        pltpu.make_async_copy(
            sums.at[it, pl.ds(0, count - 1)], sums.at[it, pl.ds(0, count - 1)], sum_send.at[it]
        ).wait()
        pltpu.make_async_copy(
            slab.at[it, pl.ds(0, across - 1)], slab.at[it, pl.ds(0, across - 1)],
            slab_send.at[it],
        ).wait()


def per_device(right_side, diagonal, features, neighbours, vertex_features, vertex_bricks):
    nrows, width, vox = features.shape
    slots = neighbours.shape[1]
    verts = vertex_bricks.shape[0]
    along, across = lax.axis_size("gx"), lax.axis_size("gy")
    count = along * across
    half = nrows // 2
    any_spec = pl.BlockSpec(memory_space=pl.ANY)
    vmem = pl.BlockSpec(memory_space=pltpu.VMEM)
    field = jax.ShapeDtypeStruct((nrows, vox), F32)
    x, r, out = pl.pallas_call(
        functools.partial(kernel, along, across, nrows, width, slots),
        out_shape=(field, field, jax.ShapeDtypeStruct((1, verts), F32)),
        in_specs=[any_spec, any_spec, any_spec, vmem, any_spec, vmem],
        out_specs=(vmem, vmem, vmem),
        scratch_shapes=[
            pltpu.VMEM((nrows, vox), F32),
            pltpu.VMEM((nrows, vox), F32),
            pltpu.VMEM((nrows, width, vox), F32),
            pltpu.VMEM((width, verts), F32),
            pltpu.VMEM((nrows, vox), F32),
            pltpu.VMEM((nrows, vox), F32),
            pltpu.VMEM((nrows, vox), F32),
            pltpu.VMEM((nrows, vox), F32),
            pltpu.VMEM((9, 32, 128), jnp.int32),
            pltpu.VMEM((ITERS, 9, half, 2 * width), F32),
            pltpu.VMEM((ITERS, across, half, 2 * width), F32),
            pltpu.VMEM((ITERS, count, 1, 128), F32),
            pltpu.VMEM((9 * nrows, 384), BF16),
            pltpu.VMEM((4 * nrows, 9 * half), BF16),
            pltpu.VMEM((across * nrows, verts), BF16),
            pltpu.SemaphoreType.DMA((3 + CHUNKS,)),
            pltpu.SemaphoreType.DMA((9,)),
            pltpu.SemaphoreType.DMA((9,)),
            pltpu.SemaphoreType.DMA((ITERS, 9)),
            pltpu.SemaphoreType.DMA((ITERS, 9)),
            pltpu.SemaphoreType.DMA((ITERS,)),
            pltpu.SemaphoreType.DMA((ITERS,)),
            pltpu.SemaphoreType.DMA((ITERS,)),
            pltpu.SemaphoreType.DMA((ITERS,)),
        ],
        compiler_params=pltpu.CompilerParams(
            collective_id=0, has_side_effects=True, vmem_limit_bytes=40 * 1024 * 1024
        ),
    )(right_side, diagonal, features, neighbours, vertex_features, vertex_bricks.reshape(1, verts))
    return x, r, out.reshape(verts)


def solution(mesh):
    rows = P(("gx", "gy"), None)
    placed = (rows, rows, P(("gx", "gy"), None, None), rows, P(None, ("gx", "gy")), P(("gx", "gy")))
    return jax.shard_map(
        per_device,
        mesh=mesh,
        in_specs=placed,
        out_specs=(rows, rows, P(("gx", "gy"))),
        check_vma=False,
    )
```

time: 374 us -> 40.5 us (0.11)
  blocking collectives: 231 us -> 0 us
  starting transfers between devices: 76 us -> 0 us
  matrix products: 32 us -> 0 us
  Pallas kernels: 0 us -> 31.4 us
  waiting for transfers between devices: 14.9 us -> 0 us
  between operations: 7.94 us -> 0.65 us
  other arithmetic: 5.32 us -> 0 us
  local copies, waits for them, and re-layouts: 3.22 us -> 8.07 us
    psum x5 -> x0, blocking collectives: 223 us -> none  [the longest x3 128 us: squares(): return lax.psum(jnp.sum(values * values), ('gx', 'gy'))]
    ppermute x28 -> x0, starting transfers between devices: 76 us -> none  [the longest x14 58 us: with_halo(): lax.ppermute(tail, axis, [(i, (i + 1) % count) for i in range(ends)])]
    dot_general x14 -> x0, matrix products: 32 us -> none  [the longest x4 22 us: coefficient(): jnp.einsum('bfv,bv->bf', features, field, precision=lax.Precision.HIGHEST)]
    pallas_call x0 -> x1, Pallas kernels: none -> 31.4 us  [per_device(): pl.pallas_call(functools.partial(kernel, along, across, nrows, width, slo...]
    ppermute x28 -> x0, waiting for transfers between devices: 14.9 us -> none  [the longest x14 14.8 us: with_halo(): lax.ppermute(tail, axis, [(i, (i + 1) % count) for i in range(ends)])]
    unnamed x17 -> x15, local copies, waits for them, and re-layouts: 0.24 us -> 8.07 us
    all_gather x1 -> x0, blocking collectives: 7.56 us -> none  [per_device(): slab_rows = lax.all_gather(surface, 'gy', axis=0, tiled=True)]
    reduce_sum x7 -> x0, other arithmetic: 4.38 us -> none  [the longest x3 1.87 us: per_device(): alpha = norm_now / lax.psum(jnp.sum(direction * image), ('gx', 'gy'))]
  transfers between devices with their start and end apart: 28 -> 0, of which waited for: 14 -> 0; matrix products, arithmetic and copies ran while one was open for 0% -> 0% of each run, Pallas kernels for 0% -> 0%
where the time goes in v1:
time: 40.5 us; the launch traced here: 40.1 us
  Pallas kernels  31.4 us (78%)
  local copies, waits for them, and re-layouts  8.07 us (20%)
  between operations  0.65 us (2%)
    pallas_call x1, Pallas kernels, per_device(): pl.pallas_call(functools.partial(kernel, along, across, nrows, width, slo...  31.4 us
    unnamed x15, local copies, waits for them, and re-layouts  8.07 us

profile of v1, /device:TPU:0, one launch (start us, length us, event | category | flops | bytes accessed | tf_op | source)
XLA Modules:
  0.0 40.1 jit_solution(6574848049620005766)
XLA Ops:
  0.6 0.0 copy-start
  0.6 2.2 %copy-done = f32[32,64,512]{2,1,0:T(8,128)S(1)} copy-done((f32[32,64,512]{2,1,0:T(8,128)S(1)}, f32[32,64,512]{2,1,0:T(8,128)}, u32[]{:S(2)}) %copy-start) | copy-done | bytes 4194328
  2.8 0.0 copy-start.1
  2.8 0.9 %copy-done.1 = f32[64,1024]{1,0:T(8,128)S(1)} copy-done((f32[64,1024]{1,0:T(8,128)S(1)}, f32[64,1024]{1,0:T(8,128)}, u32[]{:S(2)}) %copy-start.1) | copy-done | bytes 262168
  3.8 0.0 copy-start.2
  3.8 0.8 %copy-done.2 = f32[32,512]{1,0:T(8,128)S(1)} copy-done((f32[32,512]{1,0:T(8,128)S(1)}, f32[32,512]{1,0:T(8,128)}, u32[]{:S(2)}) %copy-start.2) | copy-done | bytes 65560
  4.6 0.0 copy-start.3
  4.6 0.8 %copy-done.3 = f32[32,512]{1,0:T(8,128)S(1)} copy-done((f32[32,512]{1,0:T(8,128)S(1)}, f32[32,512]{1,0:T(8,128)}, u32[]{:S(2)}) %copy-start.3) | copy-done | bytes 65560
  5.5 0.0 copy-start.4
  5.5 0.7 %copy-done.4 = s32[32,27]{1,0:T(8,128)S(1)} copy-done((s32[32,27]{1,0:T(8,128)S(1)}, s32[32,27]{1,0:T(8,128)}, u32[]{:S(2)}) %copy-start.4) | copy-done | bytes 3480
  6.2 0.0 copy-start.5
  6.2 0.7 %copy-done.5 = s32[1024]{0:T(1024)S(1)} copy-done((s32[1024]{0:T(1024)S(1)}, s32[1024]{0:T(1024)}, u32[]{:S(2)}) %copy-start.5) | copy-done | bytes 4120
  6.9 31.4 %shard_map.85 = (f32[32,512]{1,0:T(8,128)S(1)}, f32[32,512]{1,0:T(8,128)S(1)}, f32[1,1024]{1,0:T(1,128)S(1)}) custom-call(f32[32,512]{1,0:T(8,128)S(1)} %copy-done.2, f32[32,512]{1,0:T(8,128)S(1)} %copy-done.3, f32[32,64,512]{2,1,0:T(8,128)S(1)} %copy-done, s32[32,27]{1,0:T(8,128)S(1)} %copy-done.4, f32[64,1024]{1,0:T(8,128)S(1)} %copy-done.1, ...), custom_call_target="tpu_custom_call" | custom-call | tf_op jit(solution)/shard_map/pallas_call | solution.py:367
  38.2 0.6 %copy.12 = f32[32,512]{1,0:T(8,128)} copy(f32[32,512]{1,0:T(8,128)S(1)} %get-tuple-element.12) | data formatting | bytes 131072
  38.9 0.6 %copy.13 = f32[32,512]{1,0:T(8,128)} copy(f32[32,512]{1,0:T(8,128)S(1)} %get-tuple-element.13) | data formatting | bytes 131072
  39.5 0.6 %copy.14 = f32[1024]{0:T(1024)} copy(f32[1024]{0:T(1024)S(1)} %bitcast.2) | data formatting | bytes 8192
Async XLA Ops:
  0.6 2.2 %copy-start = (f32[32,64,512]{2,1,0:T(8,128)S(1)}, f32[32,64,512]{2,1,0:T(8,128)}, u32[]{:S(2)}) copy-start(f32[32,64,512]{2,1,0:T(8,128)} %f_hbm.1) | copy-start | bytes 12582916
  2.8 0.9 %copy-start.1 = (f32[64,1024]{1,0:T(8,128)S(1)}, f32[64,1024]{1,0:T(8,128)}, u32[]{:S(2)}) copy-start(f32[64,1024]{1,0:T(8,128)} %vf_hbm.1) | copy-start | bytes 786436
  3.8 0.8 %copy-start.2 = (f32[32,512]{1,0:T(8,128)S(1)}, f32[32,512]{1,0:T(8,128)}, u32[]{:S(2)}) copy-start(f32[32,512]{1,0:T(8,128)} %b_hbm.1) | copy-start | bytes 196612
  4.6 0.8 %copy-start.3 = (f32[32,512]{1,0:T(8,128)S(1)}, f32[32,512]{1,0:T(8,128)}, u32[]{:S(2)}) copy-start(f32[32,512]{1,0:T(8,128)} %d_hbm.1) | copy-start | bytes 196612
  5.5 0.7 %copy-start.4 = (s32[32,27]{1,0:T(8,128)S(1)}, s32[32,27]{1,0:T(8,128)}, u32[]{:S(2)}) copy-start(s32[32,27]{1,0:T(8,128)} %nb_ref.1) | copy-start | bytes 10372
  6.2 0.7 %copy-start.5 = (s32[1024]{0:T(1024)S(1)}, s32[1024]{0:T(1024)}, u32[]{:S(2)}) copy-start(s32[1024]{0:T(1024)} %param.11) | copy-start | bytes 12292

commit v2 on v1

--- a/solution.py
+++ b/solution.py
@@ -9,6 +9,7 @@
 
 ITERS = 3
 CHUNKS = 4
+VMEM_BYTES = 64 * 1024 * 1024
 MESH = pl.DeviceIdType.MESH
 F32 = jnp.float32
 BF16 = jnp.bfloat16
@@ -28,11 +29,11 @@
 
 def kernel(
     along, across, nrows, width, slots,
-    b_hbm, d_hbm, f_hbm, nb_ref, vf_hbm, vb_ref,
-    x_ref, r_ref, out_ref,
-    b_ref, d_ref, f_ref, vf_ref, dr_ref, p_ref, s_ref, w_ref,
+    b_hbm, d_hbm, f_hbm, nb_hbm, vf_hbm, vb_hbm,
+    x_hbm, r_hbm, out_hbm,
+    x_ref, r_ref, out_ref, b_ref, d_ref, f_ref, nb_ref, vf_ref, vb_ref, dr_ref, p_ref, s_ref, w_ref,
     tab, win, slab, sums, nwin, a4, onehot,
-    load_sem, tab_send, tab_recv, win_send, win_recv, slab_send, slab_recv, sum_send, sum_recv,
+    load_sem, store_sem, tab_send, tab_recv, win_send, win_recv, slab_send, slab_recv, sum_send, sum_recv,
 ):
     half = nrows // 2
     wrows = 9 * half
@@ -49,11 +50,15 @@
     load_vf = pltpu.make_async_copy(vf_hbm, vf_ref, load_sem.at[2])
     load_f = [
         pltpu.make_async_copy(
-            f_hbm.at[pl.ds(c * step, step)], f_ref.at[pl.ds(c * step, step)], load_sem.at[3 + c]
+            f_hbm.at[pl.ds(c * step, step)], f_ref.at[pl.ds(c * step, step)], load_sem.at[5 + c]
         )
         for c in range(CHUNKS)
     ]
+    load_nb = pltpu.make_async_copy(nb_hbm, nb_ref, load_sem.at[3])
+    load_vb = pltpu.make_async_copy(vb_hbm, vb_ref, load_sem.at[4])
+    load_nb.start()
     load_b.start()
+    load_vb.start()
     for copy in load_f:
         copy.start()
     load_d.start()
@@ -126,13 +131,10 @@
         spot = jnp.where(row >= half, wrows - half, 0) + (ox * 3 + oy) * half + row
         return jnp.where(inside, spot, -1)
 
+    load_nb.wait()
     own = nb_ref[...]
     own_t = jnp.transpose(own)
     tab[4, 0:slots, :] = jnp.concatenate([own_t] * (128 // nrows), axis=1)
-
-    pl.semaphore_wait(barrier, count - 1)
-    tab_start, tab_wait, tab_done = halo(tab, tab_send, tab_recv)
-    tab_start()
 
     spots = localize(own)
     lanes2 = iota((nrows, wrows), 1)
@@ -145,31 +147,7 @@
     a4[2 * nrows:3 * nrows, :] = n_even.astype(BF16)
     a4[3 * nrows:4 * nrows, :] = n_odd.astype(BF16)
 
-    load_b.wait()
-    lane = iota((width, 128), 1)
-
-    def reduce_coeff(b, rows, acc):
-        prod = f_ref[b] * rows
-        part = prod[:, 0:128]
-        for j in range(1, prod.shape[1] // 128):
-            part = part + prod[:, j * 128:(j + 1) * 128]
-        total = jnp.sum(part, axis=1, keepdims=True)
-        h, i = b // half, b % half
-        acc[h] = jnp.where(lane == i, total, acc[h])
-
-    def pack(acc):
-        both = jnp.concatenate(acc, axis=0)
-        return jnp.transpose(both)[0:half, :]
-
-    acc = [jnp.zeros((width, 128), F32)] * 2
-    for c in range(CHUNKS):
-        load_f[c].wait()
-        for b in range(c * step, (c + 1) * step):
-            reduce_coeff(b, b_ref[b:b + 1, :], acc)
-    win[0, 4] = pack(acc)
-    win_ops = [halo(win.at[k], win_send.at[k], win_recv.at[k]) for k in range(ITERS)]
-    win_ops[0][0]()
-
+    load_vb.wait()
     vb = vb_ref[...] - gx * (across * nrows)
     vrow = jnp.bitwise_and(vb, nrows - 1)
     code = (
@@ -181,6 +159,36 @@
         onehot[16 * g:16 * (g + 1), :] = jnp.where(block == code, 1.0, 0.0).astype(BF16)
 
     nwin[...] = jnp.zeros(nwin.shape, BF16)
+
+    pl.semaphore_wait(barrier, count - 1)
+    tab_start, tab_wait, tab_done = halo(tab, tab_send, tab_recv)
+    tab_start()
+
+    load_b.wait()
+    lane = iota((width, 128), 1)
+
+    def reduce_coeff(b, rows, acc):
+        prod = f_ref[b] * rows
+        part = prod[:, 0:128]
+        for j in range(1, prod.shape[1] // 128):
+            part = part + prod[:, j * 128:(j + 1) * 128]
+        total = jnp.sum(part, axis=1, keepdims=True)
+        h, i = b // half, b % half
+        acc[h] = jnp.where(lane == i, total, acc[h])
+
+    def pack(acc):
+        both = jnp.concatenate(acc, axis=0)
+        return jnp.transpose(both)[0:half, :]
+
+    acc = [jnp.zeros((width, 128), F32)] * 2
+    for c in range(CHUNKS):
+        load_f[c].wait()
+        for b in range(c * step, (c + 1) * step):
+            reduce_coeff(b, b_ref[b:b + 1, :], acc)
+    win[0, 4] = pack(acc)
+    win_ops = [halo(win.at[k], win_send.at[k], win_recv.at[k]) for k in range(ITERS)]
+    win_ops[0][0]()
+
     tab_wait()
     group = iota((slots, 128), 1) // nrows
     for ox in range(3):
@@ -340,7 +348,15 @@
             p_ref[...] = p
             s_ref[...] = s
     r_ref[...] = r
+    stores = [
+        pltpu.make_async_copy(a, b, store_sem.at[i])
+        for i, (a, b) in enumerate(((x_ref, x_hbm), (r_ref, r_hbm), (out_ref, out_hbm)))
+    ]
+    stores[0].start()
+    stores[1].start()
     out_ref[...] = vert[0] + alphas[2] * (vert[1] + betas[2] * vert[2])
+
+    stores[2].start()
 
     tab_done()
     for it in range(ITERS):
@@ -352,6 +368,19 @@
             slab.at[it, pl.ds(0, across - 1)], slab.at[it, pl.ds(0, across - 1)],
             slab_send.at[it],
         ).wait()
+    for copy in stores:
+        copy.wait()
+
+
+def finish(x_in, r_in, v_in, x_out, r_out, v_out, sems):
+    copies = [
+        pltpu.make_async_copy(a, b, sems.at[i])
+        for i, (a, b) in enumerate(((x_in, x_out), (r_in, r_out), (v_in, v_out)))
+    ]
+    for copy in copies:
+        copy.start()
+    for copy in copies:
+        copy.wait()
 
 
 def per_device(right_side, diagonal, features, neighbours, vertex_features, vertex_bricks):
@@ -361,19 +390,23 @@
     along, across = lax.axis_size("gx"), lax.axis_size("gy")
     count = along * across
     half = nrows // 2
-    any_spec = pl.BlockSpec(memory_space=pl.ANY)
-    vmem = pl.BlockSpec(memory_space=pltpu.VMEM)
+    hbm = pl.BlockSpec(memory_space=pltpu.HBM)
     field = jax.ShapeDtypeStruct((nrows, vox), F32)
     x, r, out = pl.pallas_call(
         functools.partial(kernel, along, across, nrows, width, slots),
         out_shape=(field, field, jax.ShapeDtypeStruct((1, verts), F32)),
-        in_specs=[any_spec, any_spec, any_spec, vmem, any_spec, vmem],
-        out_specs=(vmem, vmem, vmem),
+        in_specs=[hbm] * 6,
+        out_specs=[hbm] * 3,
         scratch_shapes=[
             pltpu.VMEM((nrows, vox), F32),
             pltpu.VMEM((nrows, vox), F32),
+            pltpu.VMEM((1, verts), F32),
+            pltpu.VMEM((nrows, vox), F32),
+            pltpu.VMEM((nrows, vox), F32),
             pltpu.VMEM((nrows, width, vox), F32),
+            pltpu.VMEM((nrows, slots), jnp.int32),
             pltpu.VMEM((width, verts), F32),
+            pltpu.VMEM((1, verts), jnp.int32),
             pltpu.VMEM((nrows, vox), F32),
             pltpu.VMEM((nrows, vox), F32),
             pltpu.VMEM((nrows, vox), F32),
@@ -385,7 +418,8 @@
             pltpu.VMEM((9 * nrows, 384), BF16),
             pltpu.VMEM((4 * nrows, 9 * half), BF16),
             pltpu.VMEM((across * nrows, verts), BF16),
-            pltpu.SemaphoreType.DMA((3 + CHUNKS,)),
+            pltpu.SemaphoreType.DMA((5 + CHUNKS,)),
+            pltpu.SemaphoreType.DMA((3,)),
             pltpu.SemaphoreType.DMA((9,)),
             pltpu.SemaphoreType.DMA((9,)),
             pltpu.SemaphoreType.DMA((ITERS, 9)),
@@ -396,9 +430,17 @@
             pltpu.SemaphoreType.DMA((ITERS,)),
         ],
         compiler_params=pltpu.CompilerParams(
-            collective_id=0, has_side_effects=True, vmem_limit_bytes=40 * 1024 * 1024
+            collective_id=0, has_side_effects=True, vmem_limit_bytes=VMEM_BYTES
         ),
     )(right_side, diagonal, features, neighbours, vertex_features, vertex_bricks.reshape(1, verts))
+    x, r, out = pl.pallas_call(
+        finish,
+        out_shape=(field, field, jax.ShapeDtypeStruct((1, verts), F32)),
+        in_specs=[hbm] * 3,
+        out_specs=[hbm] * 3,
+        scratch_shapes=[pltpu.SemaphoreType.DMA((3,))],
+        compiler_params=pltpu.CompilerParams(vmem_limit_bytes=VMEM_BYTES),
+    )(x, r, out)
     return x, r, out.reshape(verts)
 
 

time: 40.5 us -> 37.6 us (0.928)
  local copies, waits for them, and re-layouts: 8.07 us -> 0 us
  Pallas kernels: 31.4 us -> 36.7 us
    unnamed x15 -> x0, local copies, waits for them, and re-layouts: 8.07 us -> none
    pallas_call x0 -> x1, Pallas kernels: none -> 5.22 us  [per_device(): pl.pallas_call(finish, out_shape=(field, field, jax.ShapeDtypeStruct((1,...]
where the time goes in v2:
time: 37.6 us; the launch traced here: 37.3 us
  Pallas kernels  36.7 us (98%)
  between operations  0.64 us (2%)
    pallas_call x1, Pallas kernels, per_device(): pl.pallas_call(functools.partial(kernel, along, across, nrows, width, slo...  31.5 us
    pallas_call x1, Pallas kernels, per_device(): pl.pallas_call(finish, out_shape=(field, field, jax.ShapeDtypeStruct((1,...  5.22 us

profile of v2, /device:TPU:0, one launch (start us, length us, event | category | flops | bytes accessed | tf_op | source)
XLA Modules:
  0.0 37.3 jit_solution(6353658463279714761)
XLA Ops:
  0.6 31.5 %shard_map.85 = (f32[32,512]{1,0:T(8,128)}, f32[32,512]{1,0:T(8,128)}, f32[1,1024]{1,0:T(1,128)}) custom-call(f32[32,512]{1,0:T(8,128)} %b_hbm.1, f32[32,512]{1,0:T(8,128)} %d_hbm.1, f32[32,64,512]{2,1,0:T(8,128)} %f_hbm.1, s32[32,27]{1,0:T(8,128)} %nb_hbm.1, f32[64,1024]{1,0:T(8,128)} %vf_hbm.1, s32[1,1024]{1,0:T(1,128)} %bitcast.2), custom_call_target="tpu_custom_call" | custom-call | tf_op jit(solution)/shard_map/pallas_call | solution.py:395
  32.1 5.2 %shard_map.86 = (f32[32,512]{1,0:T(8,128)}, f32[32,512]{1,0:T(8,128)}, f32[1,1024]{1,0:T(1,128)}) custom-call(f32[32,512]{1,0:T(8,128)} %get-tuple-element.9.x_in, f32[32,512]{1,0:T(8,128)} %get-tuple-element.10.r_in, f32[1,1024]{1,0:T(1,128)} %get-tuple-element.11.v_in), custom_call_target="tpu_custom_call" | custom-call | tf_op jit(solution)/shard_map/pallas_call | solution.py:436

commit v3 on v2

--- a/solution.py
+++ b/solution.py
@@ -30,17 +30,16 @@
 def kernel(
     along, across, nrows, width, slots,
     b_hbm, d_hbm, f_hbm, nb_hbm, vf_hbm, vb_hbm,
-    x_hbm, r_hbm, out_hbm,
-    x_ref, r_ref, out_ref, b_ref, d_ref, f_ref, nb_ref, vf_ref, vb_ref, dr_ref, p_ref, s_ref, w_ref,
-    tab, win, slab, sums, nwin, a4, onehot,
-    load_sem, store_sem, tab_send, tab_recv, win_send, win_recv, slab_send, slab_recv, sum_send, sum_recv,
+    x_ref, r_ref, out_ref,
+    b_ref, d_ref, f_ref, nb_ref, vf_ref, vb_ref, dr_ref, p_ref, s_ref, w_ref,
+    tab, win, slab, row_sums, col_sums, nwin, a4, onehot,
+    load_sem, tab_send, tab_recv, win_send, win_recv, slab_send, slab_recv,
+    row_send, row_recv, col_send, col_recv,
 ):
     half = nrows // 2
     wrows = 9 * half
-    count = along * across
     gx = lax.axis_index("gx")
     gy = lax.axis_index("gy")
-    me = gx * across + gy
     log_rows = nrows.bit_length() - 1
     log_across = across.bit_length() - 1
 
@@ -68,25 +67,15 @@
     win[...] = jnp.zeros(win.shape, F32)
 
     barrier = pltpu.get_barrier_semaphore()
-
-    def peer(p):
-        dev = lax.rem(me + p, count)
-        return (dev // across, lax.rem(dev, across))
-
-    def over_peers(body):
-        if count <= 32:
-            for p in range(1, count):
-                body(p)
-        else:
-            def wrapped(p, carry):
-                body(p)
-                return carry
-            lax.fori_loop(1, count, wrapped, 0)
-
-    def greet(p):
-        pl.semaphore_signal(barrier, inc=1, device_id=peer(p), device_id_type=MESH)
-
-    over_peers(greet)
+    row_peers = [(gx, lax.rem(gy + p, across)) for p in range(1, across)]
+    col_peers = [(lax.rem(gx + p, along), gy) for p in range(1, along)]
+    corners = [
+        (lax.rem(gx + dx, along), lax.rem(gy + dy, across))
+        for dx in (1, along - 1) for dy in (1, across - 1)
+    ]
+    partners = row_peers + col_peers + corners
+    for device in partners:
+        pl.semaphore_signal(barrier, inc=1, device_id=device, device_id_type=MESH)
 
     places = []
     for q in range(9):
@@ -160,7 +149,7 @@
 
     nwin[...] = jnp.zeros(nwin.shape, BF16)
 
-    pl.semaphore_wait(barrier, count - 1)
+    pl.semaphore_wait(barrier, len(partners))
     tab_start, tab_wait, tab_done = halo(tab, tab_send, tab_recv)
     tab_start()
 
@@ -235,6 +224,22 @@
         for j in range(1, x.shape[1] // 128):
             res = res + tot[:, 128 * j:128 * (j + 1)]
         return jnp.sum(res, axis=0, keepdims=True)
+
+    def spread(buf, own, send, recv, peers):
+        for device in peers:
+            pltpu.make_async_remote_copy(
+                src_ref=buf.at[it, own], dst_ref=buf.at[it, own], send_sem=send.at[it],
+                recv_sem=recv.at[it], device_id=device, device_id_type=MESH,
+            ).start()
+
+    def landed(buf, k, sem, number):
+        part = buf.at[k, pl.ds(0, number)]
+        pltpu.make_async_copy(part, part, sem.at[k]).wait()
+
+    def second_stage():
+        landed(row_sums, it, row_recv, across - 1)
+        col_sums[it, gx] = jnp.sum(row_sums[it], axis=0)
+        spread(col_sums, gx, col_send, col_recv, col_peers)
 
     r = b_ref[...]
     beta = None
@@ -259,31 +264,22 @@
             ar_rows == 0, gamma_part, jnp.where(ar_rows == 1, delta_part, mu_part)
         )
         three = jnp.sum(three, axis=1, keepdims=True)
-        sums[it, me] = jnp.sum(
+        row_sums[it, gy] = jnp.sum(
             jnp.where((ar_rows == ar_lanes) & (ar_rows < 3), three, 0.0), axis=0, keepdims=True
         )
 
-        def send_sum(p, it=it):
-            pltpu.make_async_remote_copy(
-                src_ref=sums.at[it, me], dst_ref=sums.at[it, me], send_sem=sum_send.at[it],
-                recv_sem=sum_recv.at[it], device_id=peer(p), device_id_type=MESH,
-            ).start()
-
-        over_peers(send_sum)
+        spread(row_sums, gy, row_send, row_recv, row_peers)
 
         slab[it, gy] = jnp.where(
             low_lanes[0:half], first[0:half], pltpu.roll(first[half:], width, 1)
         )
-        for p in range(1, across):
-            pltpu.make_async_remote_copy(
-                src_ref=slab.at[it, gy], dst_ref=slab.at[it, gy], send_sem=slab_send.at[it],
-                recv_sem=slab_recv.at[it], device_id=(gx, lax.rem(gy + p, across)),
-                device_id_type=MESH,
-            ).start()
+        spread(slab, gy, slab_send, slab_recv, row_peers)
 
         second_t = jnp.transpose(second)[0:width, :]
         acc = [jnp.zeros((width, 128), F32)] * 2
         for b in range(nrows):
+            if it < ITERS - 1 and b == nrows * 3 // 4:
+                second_stage()
             g = jnp.sum(f_ref[b] * second_t[:, b:b + 1], axis=0, keepdims=True)
             row = dr_ref[b:b + 1, :] + g
             w_ref[b:b + 1, :] = row
@@ -293,12 +289,10 @@
             win[it + 1, 4] = pack(acc)
             win_ops[it + 1][0]()
         else:
+            second_stage()
             load_vf.wait()
             for k in range(ITERS):
-                pltpu.make_async_copy(
-                    slab.at[k, pl.ds(0, across - 1)], slab.at[k, pl.ds(0, across - 1)],
-                    slab_recv.at[k],
-                ).wait()
+                landed(slab, k, slab_recv, across - 1)
             pieces = [slab[k].reshape(across * half, 2 * width) for k in range(ITERS)]
             old = pieces[1] + betas[1] * pieces[0]
             known = alphas[0] * pieces[0] + alphas[1] * old
@@ -315,10 +309,8 @@
                     (both[0:width] + both[width:]) * vf_ref[...], axis=0, keepdims=True
                 ))
 
-        pltpu.make_async_copy(
-            sums.at[it, pl.ds(0, count - 1)], sums.at[it, pl.ds(0, count - 1)], sum_recv.at[it]
-        ).wait()
-        total = jnp.sum(sums[it], axis=0)
+        landed(col_sums, it, col_recv, along - 1)
+        total = jnp.sum(col_sums[it], axis=0)
         gamma, delta, mu = total[:, 0:1], total[:, 1:2], total[:, 2:3]
         if it == 0:
             energy = delta
@@ -348,28 +340,15 @@
             p_ref[...] = p
             s_ref[...] = s
     r_ref[...] = r
-    stores = [
-        pltpu.make_async_copy(a, b, store_sem.at[i])
-        for i, (a, b) in enumerate(((x_ref, x_hbm), (r_ref, r_hbm), (out_ref, out_hbm)))
-    ]
-    stores[0].start()
-    stores[1].start()
     out_ref[...] = vert[0] + alphas[2] * (vert[1] + betas[2] * vert[2])
 
-    stores[2].start()
 
     tab_done()
     for it in range(ITERS):
         win_ops[it][2]()
-        pltpu.make_async_copy(
-            sums.at[it, pl.ds(0, count - 1)], sums.at[it, pl.ds(0, count - 1)], sum_send.at[it]
-        ).wait()
-        pltpu.make_async_copy(
-            slab.at[it, pl.ds(0, across - 1)], slab.at[it, pl.ds(0, across - 1)],
-            slab_send.at[it],
-        ).wait()
-    for copy in stores:
-        copy.wait()
+        landed(row_sums, it, row_send, across - 1)
+        landed(col_sums, it, col_send, along - 1)
+        landed(slab, it, slab_send, across - 1)
 
 
 def finish(x_in, r_in, v_in, x_out, r_out, v_out, sems):
@@ -388,19 +367,16 @@
     slots = neighbours.shape[1]
     verts = vertex_bricks.shape[0]
     along, across = lax.axis_size("gx"), lax.axis_size("gy")
-    count = along * across
     half = nrows // 2
+    vmem = pl.BlockSpec(memory_space=pltpu.VMEM)
     hbm = pl.BlockSpec(memory_space=pltpu.HBM)
     field = jax.ShapeDtypeStruct((nrows, vox), F32)
     x, r, out = pl.pallas_call(
         functools.partial(kernel, along, across, nrows, width, slots),
         out_shape=(field, field, jax.ShapeDtypeStruct((1, verts), F32)),
         in_specs=[hbm] * 6,
-        out_specs=[hbm] * 3,
+        out_specs=[vmem] * 3,
         scratch_shapes=[
-            pltpu.VMEM((nrows, vox), F32),
-            pltpu.VMEM((nrows, vox), F32),
-            pltpu.VMEM((1, verts), F32),
             pltpu.VMEM((nrows, vox), F32),
             pltpu.VMEM((nrows, vox), F32),
             pltpu.VMEM((nrows, width, vox), F32),
@@ -414,16 +390,18 @@
             pltpu.VMEM((9, 32, 128), jnp.int32),
             pltpu.VMEM((ITERS, 9, half, 2 * width), F32),
             pltpu.VMEM((ITERS, across, half, 2 * width), F32),
-            pltpu.VMEM((ITERS, count, 1, 128), F32),
+            pltpu.VMEM((ITERS, across, 1, 128), F32),
+            pltpu.VMEM((ITERS, along, 1, 128), F32),
             pltpu.VMEM((9 * nrows, 384), BF16),
             pltpu.VMEM((4 * nrows, 9 * half), BF16),
             pltpu.VMEM((across * nrows, verts), BF16),
             pltpu.SemaphoreType.DMA((5 + CHUNKS,)),
-            pltpu.SemaphoreType.DMA((3,)),
             pltpu.SemaphoreType.DMA((9,)),
             pltpu.SemaphoreType.DMA((9,)),
             pltpu.SemaphoreType.DMA((ITERS, 9)),
             pltpu.SemaphoreType.DMA((ITERS, 9)),
+            pltpu.SemaphoreType.DMA((ITERS,)),
+            pltpu.SemaphoreType.DMA((ITERS,)),
             pltpu.SemaphoreType.DMA((ITERS,)),
             pltpu.SemaphoreType.DMA((ITERS,)),
             pltpu.SemaphoreType.DMA((ITERS,)),
@@ -436,7 +414,7 @@
     x, r, out = pl.pallas_call(
         finish,
         out_shape=(field, field, jax.ShapeDtypeStruct((1, verts), F32)),
-        in_specs=[hbm] * 3,
+        in_specs=[vmem] * 3,
         out_specs=[hbm] * 3,
         scratch_shapes=[pltpu.SemaphoreType.DMA((3,))],
         compiler_params=pltpu.CompilerParams(vmem_limit_bytes=VMEM_BYTES),

time: 37.6 us -> 36.9 us (0.981)
  Pallas kernels: 36.7 us -> 36 us
    pallas_call x1, Pallas kernels: 5.22 us -> 1.55 us  [per_device(): pl.pallas_call(finish, out_shape=(field, field, jax.ShapeDtypeStruct((1,...]
    pallas_call x1, Pallas kernels: 31.5 us -> 34.4 us  [per_device(): pl.pallas_call(functools.partial(kernel, along, across, nrows, width, slo...]
where the time goes in v3:
time: 36.9 us; the launch traced here: 36.6 us
  Pallas kernels  36 us (98%)
  between operations  0.64 us (2%)
    pallas_call x1, Pallas kernels, per_device(): pl.pallas_call(functools.partial(kernel, along, across, nrows, width, slo...  34.4 us
    pallas_call x1, Pallas kernels, per_device(): pl.pallas_call(finish, out_shape=(field, field, jax.ShapeDtypeStruct((1,...  1.55 us

profile of v3, /device:TPU:0, one launch (start us, length us, event | category | flops | bytes accessed | tf_op | source)
XLA Modules:
  0.0 36.6 jit_solution(14876384995183827786)
XLA Ops:
  0.6 34.4 %shard_map.85 = (f32[32,512]{1,0:T(8,128)}, f32[32,512]{1,0:T(8,128)}, f32[1,1024]{1,0:T(1,128)}) custom-call(f32[32,512]{1,0:T(8,128)} %b_hbm.1, f32[32,512]{1,0:T(8,128)} %d_hbm.1, f32[32,64,512]{2,1,0:T(8,128)} %f_hbm.1, s32[32,27]{1,0:T(8,128)} %nb_hbm.1, f32[64,1024]{1,0:T(8,128)} %vf_hbm.1, s32[1,1024]{1,0:T(1,128)} %bitcast.2), custom_call_target="tpu_custom_call" | custom-call | tf_op jit(solution)/shard_map/pallas_call | solution.py:374
  35.1 1.6 %shard_map.86 = (f32[32,512]{1,0:T(8,128)}, f32[32,512]{1,0:T(8,128)}, f32[1,1024]{1,0:T(1,128)}) custom-call(f32[32,512]{1,0:T(8,128)} %get-tuple-element.9.x_in, f32[32,512]{1,0:T(8,128)} %get-tuple-element.10.r_in, f32[1,1024]{1,0:T(1,128)} %get-tuple-element.11.v_in), custom_call_target="tpu_custom_call" | custom-call | tf_op jit(solution)/shard_map/pallas_call | solution.py:414

commit v4 on v3

--- a/solution.py
+++ b/solution.py
@@ -32,14 +32,16 @@
     b_hbm, d_hbm, f_hbm, nb_hbm, vf_hbm, vb_hbm,
     x_ref, r_ref, out_ref,
     b_ref, d_ref, f_ref, nb_ref, vf_ref, vb_ref, dr_ref, p_ref, s_ref, w_ref,
-    tab, win, slab, row_sums, col_sums, nwin, a4, onehot,
+    tab, win, slab, sums, nwin, a4, onehot, spread_sel, rep,
     load_sem, tab_send, tab_recv, win_send, win_recv, slab_send, slab_recv,
-    row_send, row_recv, col_send, col_recv,
+    sum_send, sum_recv,
 ):
     half = nrows // 2
     wrows = 9 * half
+    count = along * across
     gx = lax.axis_index("gx")
     gy = lax.axis_index("gy")
+    me = gx * across + gy
     log_rows = nrows.bit_length() - 1
     log_across = across.bit_length() - 1
 
@@ -68,14 +70,25 @@
 
     barrier = pltpu.get_barrier_semaphore()
     row_peers = [(gx, lax.rem(gy + p, across)) for p in range(1, across)]
-    col_peers = [(lax.rem(gx + p, along), gy) for p in range(1, along)]
-    corners = [
-        (lax.rem(gx + dx, along), lax.rem(gy + dy, across))
-        for dx in (1, along - 1) for dy in (1, across - 1)
-    ]
-    partners = row_peers + col_peers + corners
-    for device in partners:
-        pl.semaphore_signal(barrier, inc=1, device_id=device, device_id_type=MESH)
+
+    def peer(p):
+        dev = lax.rem(me + p, count)
+        return (dev // across, lax.rem(dev, across))
+
+    def over_peers(body):
+        if count <= 32:
+            for p in range(1, count):
+                body(p)
+        else:
+            def wrapped(p, carry):
+                body(p)
+                return carry
+            lax.fori_loop(1, count, wrapped, 0)
+
+    def greet(p):
+        pl.semaphore_signal(barrier, inc=1, device_id=peer(p), device_id_type=MESH)
+
+    over_peers(greet)
 
     places = []
     for q in range(9):
@@ -148,8 +161,13 @@
         onehot[16 * g:16 * (g + 1), :] = jnp.where(block == code, 1.0, 0.0).astype(BF16)
 
     nwin[...] = jnp.zeros(nwin.shape, BF16)
-
-    pl.semaphore_wait(barrier, len(partners))
+    for g in range(3 * nrows // 16):
+        shape = (16, nrows * 128)
+        spread_sel[16 * g:16 * (g + 1), :] = jnp.where(
+            jnp.right_shift(iota(shape, 1), 7) == iota(shape, 0) + 16 * g % nrows, 1.0, 0.0
+        ).astype(BF16)
+
+    pl.semaphore_wait(barrier, count - 1)
     tab_start, tab_wait, tab_done = halo(tab, tab_send, tab_recv)
     tab_start()
 
@@ -186,18 +204,21 @@
             jnp.where(group == 1, tab[3 * ox + 1, 0:slots, :], tab[3 * ox + 2, 0:slots, :]),
         )
         target = jnp.where(group < 3, localize(ids), -1)
-        rows = [jnp.broadcast_to(target[k:k + 1, :], (16, 128)) for k in range(slots)]
+        target = (target - wrows).astype(F32)
+        rows = [
+            jnp.broadcast_to(target[k:k + 1, :], (16, 128)).astype(BF16) for k in range(slots)
+        ]
         low, high = ((0, 6), (0, 9), (3, 9))[ox]
         per = (high - low) * half // 16
 
         def build(g, carry, rows=rows, low=low, per=per, ox=ox):
             h = g // per
             start = pl.multiple_of(h * wrows + low * half + (g - h * per) * 16, 16)
-            spot = iota((16, 128), 0) + start
-            hits = jnp.zeros((16, 128), F32)
+            spot = (iota((16, 128), 0) + (start - wrows)).astype(F32).astype(BF16)
+            hits = jnp.zeros((16, 128), BF16)
             for row in rows:
-                hits = jnp.where(row == spot, 1.0, hits)
-            nwin[pl.ds(start, 16), ox * 128:(ox + 1) * 128] = hits.astype(BF16)
+                hits = jnp.where(row == spot, jnp.ones((16, 128), BF16), hits)
+            nwin[pl.ds(start, 16), ox * 128:(ox + 1) * 128] = hits
             return carry
 
         lax.fori_loop(0, 2 * per, build, 0)
@@ -225,21 +246,34 @@
             res = res + tot[:, 128 * j:128 * (j + 1)]
         return jnp.sum(res, axis=0, keepdims=True)
 
-    def spread(buf, own, send, recv, peers):
-        for device in peers:
-            pltpu.make_async_remote_copy(
-                src_ref=buf.at[it, own], dst_ref=buf.at[it, own], send_sem=send.at[it],
-                recv_sem=recv.at[it], device_id=device, device_id_type=MESH,
-            ).start()
+    def send(buf, own, send_sem, recv_sem, device):
+        pltpu.make_async_remote_copy(
+            src_ref=buf.at[it, own], dst_ref=buf.at[it, own], send_sem=send_sem.at[it],
+            recv_sem=recv_sem.at[it], device_id=device, device_id_type=MESH,
+        ).start()
 
     def landed(buf, k, sem, number):
         part = buf.at[k, pl.ds(0, number)]
         pltpu.make_async_copy(part, part, sem.at[k]).wait()
 
-    def second_stage():
-        landed(row_sums, it, row_recv, across - 1)
-        col_sums[it, gx] = jnp.sum(row_sums[it], axis=0)
-        spread(col_sums, gx, col_send, col_recv, col_peers)
+    sub = iota((8, 128), 0)
+
+    def fold8(v):
+        one = []
+        for i in range(4):
+            t = jnp.where(sub < 4, v[i], v[i + 4])
+            u = jnp.where(sub < 4, v[i + 4], v[i])
+            one.append(t + pltpu.roll(u, 4, 0))
+        two = [
+            jnp.where(
+                sub % 4 < 2, one[i] + pltpu.roll(one[i], 6, 0),
+                one[i + 2] + pltpu.roll(one[i + 2], 2, 0),
+            )
+            for i in range(2)
+        ]
+        return jnp.where(
+            sub % 2 == 0, two[0] + pltpu.roll(two[0], 7, 0), two[1] + pltpu.roll(two[1], 1, 0)
+        )
 
     r = b_ref[...]
     beta = None
@@ -264,32 +298,42 @@
             ar_rows == 0, gamma_part, jnp.where(ar_rows == 1, delta_part, mu_part)
         )
         three = jnp.sum(three, axis=1, keepdims=True)
-        row_sums[it, gy] = jnp.sum(
+        sums[it, me] = jnp.sum(
             jnp.where((ar_rows == ar_lanes) & (ar_rows < 3), three, 0.0), axis=0, keepdims=True
         )
 
-        spread(row_sums, gy, row_send, row_recv, row_peers)
+        over_peers(lambda p: send(sums, me, sum_send, sum_recv, peer(p)))
 
         slab[it, gy] = jnp.where(
             low_lanes[0:half], first[0:half], pltpu.roll(first[half:], width, 1)
         )
-        spread(slab, gy, slab_send, slab_recv, row_peers)
-
-        second_t = jnp.transpose(second)[0:width, :]
+        for device in row_peers:
+            send(slab, gy, slab_send, slab_recv, device)
+
+        thirds = jnp.concatenate([t.astype(F32) for t in split3(second)], axis=0)
+        thirds = jnp.transpose(thirds)[0:width, :].astype(BF16)
+        for c in range(0, nrows * 128, 512):
+            rep[:, c:c + 512] = jnp.dot(
+                thirds, spread_sel[:, c:c + 512], preferred_element_type=F32
+            )
         acc = [jnp.zeros((width, 128), F32)] * 2
-        for b in range(nrows):
-            if it < ITERS - 1 and b == nrows * 3 // 4:
-                second_stage()
-            g = jnp.sum(f_ref[b] * second_t[:, b:b + 1], axis=0, keepdims=True)
-            row = dr_ref[b:b + 1, :] + g
-            w_ref[b:b + 1, :] = row
+        for g in range(0, nrows, 8):
+            tiles = f_ref.shape[2] // 128
+            parts = [[None] * 8 for _ in range(tiles)]
+            for b in range(8):
+                factor = rep[:, (g + b) * 128:(g + b + 1) * 128]
+                for j in range(tiles):
+                    prod = f_ref[g + b, :, j * 128:(j + 1) * 128] * factor
+                    parts[j][b] = jnp.sum(prod.reshape(width // 8, 8, 128), axis=0)
+            image = jnp.concatenate([fold8(part) for part in parts], axis=1)
+            w_ref[g:g + 8, :] = dr_ref[g:g + 8, :] + image
             if it < ITERS - 1:
-                reduce_coeff(b, row, acc)
+                for b in range(g, g + 8):
+                    reduce_coeff(b, w_ref[b:b + 1, :], acc)
         if it < ITERS - 1:
             win[it + 1, 4] = pack(acc)
             win_ops[it + 1][0]()
         else:
-            second_stage()
             load_vf.wait()
             for k in range(ITERS):
                 landed(slab, k, slab_recv, across - 1)
@@ -309,8 +353,8 @@
                     (both[0:width] + both[width:]) * vf_ref[...], axis=0, keepdims=True
                 ))
 
-        landed(col_sums, it, col_recv, along - 1)
-        total = jnp.sum(col_sums[it], axis=0)
+        landed(sums, it, sum_recv, count - 1)
+        total = jnp.sum(sums[it], axis=0)
         gamma, delta, mu = total[:, 0:1], total[:, 1:2], total[:, 2:3]
         if it == 0:
             energy = delta
@@ -346,8 +390,7 @@
     tab_done()
     for it in range(ITERS):
         win_ops[it][2]()
-        landed(row_sums, it, row_send, across - 1)
-        landed(col_sums, it, col_send, along - 1)
+        landed(sums, it, sum_send, count - 1)
         landed(slab, it, slab_send, across - 1)
 
 
@@ -367,6 +410,7 @@
     slots = neighbours.shape[1]
     verts = vertex_bricks.shape[0]
     along, across = lax.axis_size("gx"), lax.axis_size("gy")
+    count = along * across
     half = nrows // 2
     vmem = pl.BlockSpec(memory_space=pltpu.VMEM)
     hbm = pl.BlockSpec(memory_space=pltpu.HBM)
@@ -390,18 +434,17 @@
             pltpu.VMEM((9, 32, 128), jnp.int32),
             pltpu.VMEM((ITERS, 9, half, 2 * width), F32),
             pltpu.VMEM((ITERS, across, half, 2 * width), F32),
-            pltpu.VMEM((ITERS, across, 1, 128), F32),
-            pltpu.VMEM((ITERS, along, 1, 128), F32),
+            pltpu.VMEM((ITERS, count, 1, 128), F32),
             pltpu.VMEM((9 * nrows, 384), BF16),
             pltpu.VMEM((4 * nrows, 9 * half), BF16),
             pltpu.VMEM((across * nrows, verts), BF16),
+            pltpu.VMEM((3 * nrows, nrows * 128), BF16),
+            pltpu.VMEM((width, nrows * 128), F32),
             pltpu.SemaphoreType.DMA((5 + CHUNKS,)),
             pltpu.SemaphoreType.DMA((9,)),
             pltpu.SemaphoreType.DMA((9,)),
             pltpu.SemaphoreType.DMA((ITERS, 9)),
             pltpu.SemaphoreType.DMA((ITERS, 9)),
-            pltpu.SemaphoreType.DMA((ITERS,)),
-            pltpu.SemaphoreType.DMA((ITERS,)),
             pltpu.SemaphoreType.DMA((ITERS,)),
             pltpu.SemaphoreType.DMA((ITERS,)),
             pltpu.SemaphoreType.DMA((ITERS,)),

time: 36.9 us -> 31.3 us (0.85)
  Pallas kernels: 36 us -> 30.4 us
    pallas_call x1, Pallas kernels: 34.4 us -> 28.9 us  [per_device(): pl.pallas_call(functools.partial(kernel, along, across, nrows, width, slo...]
where the time goes in v4:
time: 31.3 us; the launch traced here: 31.1 us
  Pallas kernels  30.4 us (97%)
  between operations  0.64 us (2%)
    pallas_call x1, Pallas kernels, per_device(): pl.pallas_call(functools.partial(kernel, along, across, nrows, width, slo...  28.9 us
    pallas_call x1, Pallas kernels, per_device(): pl.pallas_call(finish, out_shape=(field, field, jax.ShapeDtypeStruct((1,...  1.55 us

profile of v4, /device:TPU:0, one launch (start us, length us, event | category | flops | bytes accessed | tf_op | source)
XLA Modules:
  0.0 31.1 jit_solution(11639003885312837577)
XLA Ops:
  0.6 28.9 %shard_map.85 = (f32[32,512]{1,0:T(8,128)}, f32[32,512]{1,0:T(8,128)}, f32[1,1024]{1,0:T(1,128)}) custom-call(f32[32,512]{1,0:T(8,128)} %b_hbm.1, f32[32,512]{1,0:T(8,128)} %d_hbm.1, f32[32,64,512]{2,1,0:T(8,128)} %f_hbm.1, s32[32,27]{1,0:T(8,128)} %nb_hbm.1, f32[64,1024]{1,0:T(8,128)} %vf_hbm.1, s32[1,1024]{1,0:T(1,128)} %bitcast.2), custom_call_target="tpu_custom_call" | custom-call | tf_op jit(solution)/shard_map/pallas_call | solution.py:418
  29.5 1.6 %shard_map.86 = (f32[32,512]{1,0:T(8,128)}, f32[32,512]{1,0:T(8,128)}, f32[1,1024]{1,0:T(1,128)}) custom-call(f32[32,512]{1,0:T(8,128)} %get-tuple-element.9.x_in, f32[32,512]{1,0:T(8,128)} %get-tuple-element.10.r_in, f32[1,1024]{1,0:T(1,128)} %get-tuple-element.11.v_in), custom_call_target="tpu_custom_call" | custom-call | tf_op jit(solution)/shard_map/pallas_call | solution.py:457

commit v5 on v4

--- a/solution.py
+++ b/solution.py
@@ -9,7 +9,7 @@
 
 ITERS = 3
 CHUNKS = 4
-VMEM_BYTES = 64 * 1024 * 1024
+VMEM_BYTES = 40 * 1024 * 1024
 MESH = pl.DeviceIdType.MESH
 F32 = jnp.float32
 BF16 = jnp.bfloat16
@@ -32,7 +32,7 @@
     b_hbm, d_hbm, f_hbm, nb_hbm, vf_hbm, vb_hbm,
     x_ref, r_ref, out_ref,
     b_ref, d_ref, f_ref, nb_ref, vf_ref, vb_ref, dr_ref, p_ref, s_ref, w_ref,
-    tab, win, slab, sums, nwin, a4, onehot, spread_sel, rep,
+    tab, win, slab, sums, nwin, a4, onehot, spread_sel, rep, lane_sel, part_hi, part_lo,
     load_sem, tab_send, tab_recv, win_send, win_recv, slab_send, slab_recv,
     sum_send, sum_recv,
 ):
@@ -161,6 +161,9 @@
         onehot[16 * g:16 * (g + 1), :] = jnp.where(block == code, 1.0, 0.0).astype(BF16)
 
     nwin[...] = jnp.zeros(nwin.shape, BF16)
+    shape = (128, 128)
+    for i in range(half):
+        lane_sel[i * 128:(i + 1) * 128, :] = jnp.where(iota(shape, 1) == i, 1.0, 0.0).astype(BF16)
     for g in range(3 * nrows // 16):
         shape = (16, nrows * 128)
         spread_sel[16 * g:16 * (g + 1), :] = jnp.where(
@@ -172,27 +175,31 @@
     tab_start()
 
     load_b.wait()
-    lane = iota((width, 128), 1)
-
-    def reduce_coeff(b, rows, acc):
+
+    def reduce_coeff(b, rows):
         prod = f_ref[b] * rows
         part = prod[:, 0:128]
         for j in range(1, prod.shape[1] // 128):
             part = part + prod[:, j * 128:(j + 1) * 128]
-        total = jnp.sum(part, axis=1, keepdims=True)
-        h, i = b // half, b % half
-        acc[h] = jnp.where(lane == i, total, acc[h])
-
-    def pack(acc):
-        both = jnp.concatenate(acc, axis=0)
-        return jnp.transpose(both)[0:half, :]
-
-    acc = [jnp.zeros((width, 128), F32)] * 2
+        hi = part.astype(BF16)
+        part_hi[:, b * 128:(b + 1) * 128] = hi
+        part_lo[:, b * 128:(b + 1) * 128] = (part - hi.astype(F32)).astype(BF16)
+
+    def pack():
+        both = []
+        for h in range(2):
+            span = slice(h * half * 128, (h + 1) * half * 128)
+            both.append(
+                jnp.dot(part_hi[:, span], lane_sel[...], preferred_element_type=F32)
+                + jnp.dot(part_lo[:, span], lane_sel[...], preferred_element_type=F32)
+            )
+        return jnp.transpose(jnp.concatenate(both, axis=0))[0:half, :]
+
     for c in range(CHUNKS):
         load_f[c].wait()
         for b in range(c * step, (c + 1) * step):
-            reduce_coeff(b, b_ref[b:b + 1, :], acc)
-    win[0, 4] = pack(acc)
+            reduce_coeff(b, b_ref[b:b + 1, :])
+    win[0, 4] = pack()
     win_ops = [halo(win.at[k], win_send.at[k], win_recv.at[k]) for k in range(ITERS)]
     win_ops[0][0]()
 
@@ -316,7 +323,6 @@
             rep[:, c:c + 512] = jnp.dot(
                 thirds, spread_sel[:, c:c + 512], preferred_element_type=F32
             )
-        acc = [jnp.zeros((width, 128), F32)] * 2
         for g in range(0, nrows, 8):
             tiles = f_ref.shape[2] // 128
             parts = [[None] * 8 for _ in range(tiles)]
@@ -329,9 +335,9 @@
             w_ref[g:g + 8, :] = dr_ref[g:g + 8, :] + image
             if it < ITERS - 1:
                 for b in range(g, g + 8):
-                    reduce_coeff(b, w_ref[b:b + 1, :], acc)
+                    reduce_coeff(b, w_ref[b:b + 1, :])
         if it < ITERS - 1:
-            win[it + 1, 4] = pack(acc)
+            win[it + 1, 4] = pack()
             win_ops[it + 1][0]()
         else:
             load_vf.wait()
@@ -440,6 +446,9 @@
             pltpu.VMEM((across * nrows, verts), BF16),
             pltpu.VMEM((3 * nrows, nrows * 128), BF16),
             pltpu.VMEM((width, nrows * 128), F32),
+            pltpu.VMEM((half * 128, 128), BF16),
+            pltpu.VMEM((width, nrows * 128), BF16),
+            pltpu.VMEM((width, nrows * 128), BF16),
             pltpu.SemaphoreType.DMA((5 + CHUNKS,)),
             pltpu.SemaphoreType.DMA((9,)),
             pltpu.SemaphoreType.DMA((9,)),
@@ -453,7 +462,13 @@
         compiler_params=pltpu.CompilerParams(
             collective_id=0, has_side_effects=True, vmem_limit_bytes=VMEM_BYTES
         ),
-    )(right_side, diagonal, features, neighbours, vertex_features, vertex_bricks.reshape(1, verts))
+    )(*[
+        pltpu.with_memory_space_constraint(a, pltpu.HBM)
+        for a in (
+            right_side, diagonal, features, neighbours, vertex_features,
+            vertex_bricks.reshape(1, verts),
+        )
+    ])
     x, r, out = pl.pallas_call(
         finish,
         out_shape=(field, field, jax.ShapeDtypeStruct((1, verts), F32)),

time: 31.3 us -> 30.3 us (0.968)
  Pallas kernels: 30.4 us -> 29.4 us
    pallas_call x1, Pallas kernels: 1.55 us -> 0.68 us  [per_device(): pl.pallas_call(finish, out_shape=(field, field, jax.ShapeDtypeStruct((1,...]
where the time goes in v5:
time: 30.3 us; the launch traced here: 30.1 us
  Pallas kernels  29.4 us (97%)
  between operations  0.64 us (2%)
    pallas_call x1, Pallas kernels, per_device(): pl.pallas_call(functools.partial(kernel, along, across, nrows, width, slo...  28.7 us
    pallas_call x1, Pallas kernels, per_device(): pl.pallas_call(finish, out_shape=(field, field, jax.ShapeDtypeStruct((1,...  0.68 us

profile of v5, /device:TPU:0, one launch (start us, length us, event | category | flops | bytes accessed | tf_op | source)
XLA Modules:
  0.0 30.1 jit_solution(15841992382818468811)
XLA Ops:
  0.6 28.7 %shard_map.85 = (f32[32,512]{1,0:T(8,128)S(1)}, f32[32,512]{1,0:T(8,128)S(1)}, f32[1,1024]{1,0:T(1,128)S(1)}) custom-call(f32[32,512]{1,0:T(8,128)} %b_hbm.1, f32[32,512]{1,0:T(8,128)} %d_hbm.1, f32[32,64,512]{2,1,0:T(8,128)} %f_hbm.1, s32[32,27]{1,0:T(8,128)} %nb_hbm.1, f32[64,1024]{1,0:T(8,128)} %vf_hbm.1, s32[1,1024]{1,0:T(1,128)} %bitcast.2), custom_call_target="tpu_custom_call" | custom-call | tf_op jit(solution)/shard_map/pallas_call | solution.py:424
  29.4 0.7 %shard_map.86 = (f32[32,512]{1,0:T(8,128)}, f32[32,512]{1,0:T(8,128)}, f32[1,1024]{1,0:T(1,128)}) custom-call(f32[32,512]{1,0:T(8,128)S(1)} %get-tuple-element.9.x_in, f32[32,512]{1,0:T(8,128)S(1)} %get-tuple-element.10.r_in, f32[1,1024]{1,0:T(1,128)S(1)} %get-tuple-element.11.v_in), custom_call_target="tpu_custom_call" | custom-call | tf_op jit(solution)/shard_map/pallas_call | solution.py:472

commit v6 on v4

--- a/solution.py
+++ b/solution.py
@@ -9,7 +9,7 @@
 
 ITERS = 3
 CHUNKS = 4
-VMEM_BYTES = 64 * 1024 * 1024
+VMEM_BYTES = 40 * 1024 * 1024
 MESH = pl.DeviceIdType.MESH
 F32 = jnp.float32
 BF16 = jnp.bfloat16
@@ -453,7 +453,13 @@
         compiler_params=pltpu.CompilerParams(
             collective_id=0, has_side_effects=True, vmem_limit_bytes=VMEM_BYTES
         ),
-    )(right_side, diagonal, features, neighbours, vertex_features, vertex_bricks.reshape(1, verts))
+    )(*[
+        pltpu.with_memory_space_constraint(a, pltpu.HBM)
+        for a in (
+            right_side, diagonal, features, neighbours, vertex_features,
+            vertex_bricks.reshape(1, verts),
+        )
+    ])
     x, r, out = pl.pallas_call(
         finish,
         out_shape=(field, field, jax.ShapeDtypeStruct((1, verts), F32)),

time: 31.3 us -> 29.8 us (0.952)
  Pallas kernels: 30.4 us -> 28.9 us
    pallas_call x1, Pallas kernels: 1.55 us -> 0.68 us  [per_device(): pl.pallas_call(finish, out_shape=(field, field, jax.ShapeDtypeStruct((1,...]
    pallas_call x1, Pallas kernels: 28.9 us -> 28.2 us  [per_device(): pl.pallas_call(functools.partial(kernel, along, across, nrows, width, slo...]
where the time goes in v6:
time: 29.8 us; the launch traced here: 29.6 us
  Pallas kernels  28.9 us (97%)
  between operations  0.64 us (2%)
    pallas_call x1, Pallas kernels, per_device(): pl.pallas_call(functools.partial(kernel, along, across, nrows, width, slo...  28.2 us
    pallas_call x1, Pallas kernels, per_device(): pl.pallas_call(finish, out_shape=(field, field, jax.ShapeDtypeStruct((1,...  0.68 us

profile of v6, /device:TPU:0, one launch (start us, length us, event | category | flops | bytes accessed | tf_op | source)
XLA Modules:
  0.0 29.6 jit_solution(16494224232407264384)
XLA Ops:
  0.6 28.2 %shard_map.85 = (f32[32,512]{1,0:T(8,128)S(1)}, f32[32,512]{1,0:T(8,128)S(1)}, f32[1,1024]{1,0:T(1,128)S(1)}) custom-call(f32[32,512]{1,0:T(8,128)} %b_hbm.1, f32[32,512]{1,0:T(8,128)} %d_hbm.1, f32[32,64,512]{2,1,0:T(8,128)} %f_hbm.1, s32[32,27]{1,0:T(8,128)} %nb_hbm.1, f32[64,1024]{1,0:T(8,128)} %vf_hbm.1, s32[1,1024]{1,0:T(1,128)} %bitcast.2), custom_call_target="tpu_custom_call" | custom-call | tf_op jit(solution)/shard_map/pallas_call | solution.py:418
  28.9 0.7 %shard_map.86 = (f32[32,512]{1,0:T(8,128)}, f32[32,512]{1,0:T(8,128)}, f32[1,1024]{1,0:T(1,128)}) custom-call(f32[32,512]{1,0:T(8,128)S(1)} %get-tuple-element.9.x_in, f32[32,512]{1,0:T(8,128)S(1)} %get-tuple-element.10.r_in, f32[1,1024]{1,0:T(1,128)S(1)} %get-tuple-element.11.v_in), custom_call_target="tpu_custom_call" | custom-call | tf_op jit(solution)/shard_map/pallas_call | solution.py:463
